TPU v7x, 32 devices: a whole 2x2x4 slice. The times are simulated.
32 devices in a mesh: pair: 8 (over z, y), red: 4 (over x, core).
Axes of the slice: x: 2, y: 2, z: 4, core: 2. Of those that a mesh axis runs over, the one named last changes fastest.
Arguments:
- amplitudes: bfloat16 [64, 64, 8192], P('pair', None, 'red'), may hold values from -6 to 6
- integrals: bfloat16 [8192, 1024], P('red'), may hold values from -0.1875 to 0.1875
- occ_irrep: int32 [64], replicated, may hold values from 0 to 7
- vir_irrep: int32 [512], replicated, may hold values from 0 to 7, as said below
- cd_orbitals: int32 [2, 8192], P(None, 'red'), may hold values from 0 to 511
- ab_orbitals: int32 [2, 1024], P(None, 'pair'), may hold values from 0 to 511, as said below
Outputs:
- residual: bfloat16 [64, 64, 1024], P(None, 'red', 'pair')
Inputs may be any that keep to these rules, and one draw needn't show every extreme that they name: `vir_irrep`: D2h irrep labels; each label is held by exactly 64 virtual orbitals. `occ_irrep`: D2h irrep labels. `cd_orbitals`: indices of virtual orbitals. `ab_orbitals`: indices of virtual orbitals; the slab pairs m with m // 128 equal come as 8 blocks of 16 pairs, and ab_irrep[m] = (m % 128) // 16.
All inputs are finite; a program needn't handle non-finite values.
Results may differ from a plain program's by a relative error of at most 0.001.
Values may be sent and summed in bfloat16 or wider, within the bound.
No kernel may reach another device: no remote copies, remote signals or barrier semaphores. Data moves between devices by JAX's collectives and lax.ppermute only.
A program may use at most 192 MiB of HBM per device.

v0:
```python
import jax
import jax.numpy as jnp
from jax import lax
from jax.sharding import PartitionSpec as P


def pair_labels(orbitals, vir_irrep):
    labels = lax.broadcasted_iota(jnp.int32, (1, vir_irrep.shape[0]), 1)
    first_label = jnp.sum(jnp.where(orbitals[0][:, None] == labels, vir_irrep[None, :], 0), axis=1)
    second_label = jnp.sum(jnp.where(orbitals[1][:, None] == labels, vir_irrep[None, :], 0), axis=1)
    return jnp.bitwise_xor(first_label, second_label)


def local(amplitudes, integrals, occ_irrep, vir_irrep, cd_orbitals, ab_orbitals):
    own_rows = amplitudes.shape[0]
    occupied = amplitudes.shape[1]
    slab_width = integrals.shape[1]
    first_row = lax.axis_index("pair") * own_rows
    own_irrep = lax.dynamic_slice_in_dim(occ_irrep, first_row, own_rows, 0)
    pair_irrep = jnp.bitwise_xor(own_irrep[:, None], occ_irrep[None, :])
    cd_irrep = pair_labels(cd_orbitals, vir_irrep)
    masked = jnp.where(
        pair_irrep[:, :, None] == cd_irrep[None, None, :],
        amplitudes,
        jnp.zeros((), amplitudes.dtype),
    )
    partial_sums = jnp.dot(
        masked.reshape(own_rows * occupied, masked.shape[2]),
        integrals,
        preferred_element_type=jnp.float32,
    )
    partial_sums = partial_sums.reshape(own_rows, occupied, slab_width)
    moved = lax.all_to_all(partial_sums, "pair", split_axis=2, concat_axis=0, tiled=True)
    summed = lax.psum_scatter(moved, "red", scatter_dimension=1, tiled=True)
    j_rows = summed.shape[1]
    j_irrep = lax.dynamic_slice_in_dim(occ_irrep, lax.axis_index("red") * j_rows, j_rows, 0)
    out_irrep = jnp.bitwise_xor(occ_irrep[:, None], j_irrep[None, :])
    ab_irrep = pair_labels(ab_orbitals, vir_irrep)
    kept = jnp.where(
        out_irrep[:, :, None] == ab_irrep[None, None, :], summed, jnp.zeros((), summed.dtype)
    )
    return kept.astype(jnp.bfloat16)


def solution(mesh):
    in_specs = (P("pair", None, "red"), P("red", None), P(), P(), P(None, "red"), P(None, "pair"))
    out_specs = P(None, "red", "pair")
    return jax.shard_map(local, mesh=mesh, in_specs=in_specs, out_specs=out_specs, check_vma=False)
```

profile of v0, /device:TPU:0, one launch (start us, length us, event | category | flops | bytes accessed | tf_op | source)
XLA Modules:
  0.0 135.0 jit_solution(4878765233480523727)
XLA Ops:
  6.5 0.0 reduce-scatter.2.cloned.1.call-start
  6.5 0.7 dynamic_slice.7
  7.3 0.7 broadcast_xor_fusion.1
  8.0 0.8 fusion.6
  8.8 2.3 %select_reduce_fusion = (s32[2048]{0:T(1024)S(1)}, s32[2048]{0:T(1024)S(1)}) fusion(s32[2048]{0:T(1024)S(1)} %bitcast.19, s32[512]{0:T(512)} %param.9, s32[2048]{0:T(1024)S(1)} %bitcast.18), kind=kLoop, calls=%fused_computation.2 | loop fusion | flops 6287360 | bytes 34816 | tf_op jit(solution)/shard_map/reduce_sum | solution.py:10
  11.1 5.2 %fusion = f32[8,64,1024]{2,1,0:T(8,128)S(1)} fusion(bf16[2048,1024]{1,0:T(8,128)(2,1)} %param.7, bf16[8,64,2048]{2,1,0:T(8,128)(2,1)} %param.6, s32[2048]{0:T(1024)S(1)} %xor.55, s32[8,64]{1,0:T(8,128)S(1)} %broadcast_xor_fusion.1), kind=kOutput, calls=%fused_computation | convolution fusion | flops 2149580800 | bytes 8398848 | tf_op jit(solution)/shard_map/dot_general | solution.py:27
  16.3 2.7 %copy.10 = f32[8,64,1024]{1,0,2:T(8,128)} copy(f32[8,64,1024]{2,1,0:T(8,128)S(1)} %fusion) | data formatting | bytes 4194304 | tf_op jit(solution)/shard_map/dot_general | solution.py:27
  19.1 5.9 %reshape.74 = f32[8,1,65536]{2,1,0:T(1,128)S(1)} reshape(f32[1024,8,64]{2,1,0:T(8,128)} %bitcast.15) | data formatting | bytes 4194304
  25.0 55.4 %all_to_all.18 = f32[8,1,65536]{2,1,0:T(1,128)} all-to-all(f32[8,1,65536]{2,1,0:T(1,128)S(1)} %reshape.74), channel_id=1, replica_groups=mesh['pair'=8,'red'=4] {'pair'}, dimensions={0} | all-to-all | bytes 4194304 | tf_op jit(solution)/shard_map/all_to_all | solution.py:33
  80.4 0.5 broadcast.39
  81.0 7.2 %reduce = f32[8,65536]{1,0:T(8,128)S(1)} reduce(f32[8,1,65536]{2,1,0:T(1,128)} %all_to_all.18, f32[]{:T(128)} %broadcast.39), dimensions={1}, to_apply=%all_to_all.13.reduce_sub_computation | reduce | bytes 4194308 | tf_op jit(solution)/shard_map/all_to_all | solution.py:33
  88.2 3.6 %reshape.75 = f32[1024,8,64]{2,1,0:T(8,128)} reshape(f32[8,65536]{1,0:T(8,128)S(1)} %reduce) | data formatting | bytes 4194304
  91.8 0.0 copy-start.1
  91.8 0.0 copy-start.2
  91.8 0.0 copy-start
  91.8 3.9 %copy.11 = f32[8,8,64,128]{3,2,1,0:T(8,128)} copy(f32[8,8,64,128]{2,1,3,0:T(8,128)} %bitcast.16) | data formatting | bytes 4194304 | tf_op jit(solution)/shard_map/all_to_all | solution.py:33
  95.6 0.0 reduce-scatter.2.cloned.1.call-update
  95.7 0.0 copy-done.1
  95.7 0.1 dynamic_slice.6
  95.8 0.0 copy-done.2
  95.8 0.0 copy-done
  95.8 0.2 select_reduce_fusion.2
  96.0 0.1 broadcast_xor_fusion
  96.1 30.2 %reduce-scatter.2.cloned.1.call-done = f32[64,16,128]{2,1,0:T(8,128)} async-done(((f32[64,64,128]{2,1,0:T(8,128)}), f32[64,16,128]{2,1,0:T(8,128)}) %reduce-scatter.2.cloned.1.call-update) | async-done | bytes 524304 | tf_op jit(solution)/shard_map/reduce_scatter | solution.py:34
  126.2 1.9 %select_convert_fusion = bf16[64,16,128]{2,1,0:T(8,128)(2,1)} fusion(f32[64,16,128]{2,1,0:T(8,128)} %reduce-scatter.2.cloned.1.call-done, s32[128]{0:T(128)S(1)} %xor.51, s32[64,16]{1,0:T(8,128)S(1)} %broadcast_xor_fusion), kind=kLoop, calls=%fused_computation.10 | loop fusion | flops 262144 | bytes 791040 | tf_op jit(solution)/shard_map/convert_element_type | solution.py:42
  (3 shorter events, 0.0 us)
Async XLA Ops:
  6.5 119.7 %reduce-scatter.2.cloned.1.call-start = ((), (), s32[]{:S(2)}) async-start(), calls=%async_computation.2 | async-start | bytes 2621440 | tf_op jit(solution)/shard_map/reduce_scatter | solution.py:34
  91.8 3.9 %copy-start.1 = (s32[64]{0:T(128)S(1)}, s32[64]{0:T(128)}, u32[]{:S(2)}) copy-start(s32[64]{0:T(128)} %param.8) | copy-start | bytes 772
  91.8 4.0 %copy-start.2 = (s32[2,128]{1,0:T(2,128)S(1)}, s32[2,128]{1,0:T(2,128)}, u32[]{:S(2)}) copy-start(s32[2,128]{1,0:T(2,128)} %param.11) | copy-start | bytes 3076
  91.8 4.0 %copy-start = (s32[512]{0:T(512)S(1)}, s32[512]{0:T(512)}, u32[]{:S(2)}) copy-start(s32[512]{0:T(512)} %param.9) | copy-start | bytes 6148
Sparse Core Ops, SparseCore 0:
  95.8 30.4 reduce-scatter.1
where the time goes:
time: 135 us
  blocking collectives  55.4 us (41%)
  waiting for transfers between devices  30.2 us (22%)
  local copies, waits for them, and re-layouts  18.3 us (14%)
  between operations  13.5 us (10%)
  other arithmetic  12.5 us (9%)
  matrix products  5.21 us (4%)
    all_to_all x1, blocking collectives, local(): lax.all_to_all(partial_sums, 'pair', split_axis=2, concat_axis=0, tiled=T...  55.4 us
    reduce_scatter x1, waiting for transfers between devices, local(): summed = lax.psum_scatter(moved, 'red', scatter_dimension=1, tiled=True)  30.2 us
    unnamed x8, local copies, waits for them, and re-layouts  9.53 us
    all_to_all x1, other arithmetic, local(): lax.all_to_all(partial_sums, 'pair', split_axis=2, concat_axis=0, tiled=T...  7.22 us
    dot_general x1, matrix products, local(): jnp.dot(masked.reshape(own_rows * occupied, masked.shape[2]), integrals,...  5.21 us
    all_to_all x2, local copies, waits for them, and re-layouts, local(): lax.all_to_all(partial_sums, 'pair', split_axis=2, concat_axis=0, tiled=T...  4.38 us
    dot_general x1, local copies, waits for them, and re-layouts, local(): jnp.dot(masked.reshape(own_rows * occupied, masked.shape[2]), integrals,...  2.74 us
  transfers between devices with their start and end apart: 1, of which 1 were waited for; matrix products, arithmetic and copies ran while one was open for 0% of the time, Pallas kernels for 0%

commit v1 on v0

v1 whole, which is shorter than its diff:
```python
import functools

import jax
import jax.numpy as jnp
from jax import lax
from jax.experimental import pallas as pl
from jax.experimental.pallas import tpu as pltpu
from jax.sharding import PartitionSpec as P

LABELS = 8
LANES = 128
BLOCK = LANES // LABELS
F32, BF16, I32 = jnp.float32, jnp.bfloat16, jnp.int32


def pair_labels(orbitals, vir_irrep):
    labels = lax.broadcasted_iota(I32, (1, vir_irrep.shape[0]), 1)
    first = jnp.sum(jnp.where(orbitals[0][:, None] == labels, vir_irrep[None, :], 0), axis=1)
    second = jnp.sum(jnp.where(orbitals[1][:, None] == labels, vir_irrep[None, :], 0), axis=1)
    return jnp.bitwise_xor(first, second)


def general(amplitudes, integrals, occ_irrep, vir_irrep, cd_orbitals, ab_orbitals):
    own_rows, occupied, depth = amplitudes.shape
    width = ab_orbitals.shape[1]
    owners = integrals.shape[1] // width
    block = width // LABELS
    own_irrep = lax.dynamic_slice_in_dim(occ_irrep, lax.axis_index("pair") * own_rows, own_rows, 0)
    pair_irrep = jnp.bitwise_xor(own_irrep[:, None], occ_irrep[None, :])
    cd_irrep = pair_labels(cd_orbitals, vir_irrep)
    masked = jnp.where(pair_irrep[:, :, None] == cd_irrep, amplitudes, jnp.zeros((), BF16))
    sums = jnp.dot(
        masked.reshape(own_rows * occupied, depth), integrals, preferred_element_type=F32
    ).reshape(own_rows, occupied, owners, LABELS, block)
    label = lax.broadcasted_iota(I32, (LABELS, 1), 0)
    kept = jnp.where(pair_irrep[:, :, None, None, None] == label, sums, 0.0).sum(axis=3)
    summed = lax.psum_scatter(kept, "red", scatter_dimension=1, tiled=True)
    moved = lax.all_to_all(
        summed.astype(BF16), "pair", split_axis=2, concat_axis=0, tiled=True
    )[:, :, 0, None, :]
    j_rows = moved.shape[1]
    j_irrep = lax.dynamic_slice_in_dim(occ_irrep, lax.axis_index("red") * j_rows, j_rows, 0)
    out_irrep = jnp.bitwise_xor(occ_irrep[:, None], j_irrep[None, :])
    out = jnp.where(out_irrep[:, :, None, None] == label, moved, jnp.zeros((), BF16))
    return out.reshape(occupied, j_rows, width)


OWNERS = 8
REDS = 4
V_CHUNKS = 2


def place(offset):
    bit = [(offset >> b) & 1 for b in range(5)]
    odd = bit[0] ^ bit[1] ^ bit[2] ^ bit[3] ^ bit[4]
    return (((odd * 2 + bit[1]) * 2 + bit[2]) * 2 + bit[3]) * 2 + bit[4]


def pick(vectors, shift_bits):
    for b in range(3):
        vectors = [
            jnp.where(shift_bits[b], vectors[(d + 2**b) % 8], vectors[d]) for d in range(8)
        ]
    return vectors


def turn(vector, blocks):
    return pltpu.roll(vector, blocks % LABELS * BLOCK, 1) if blocks % LABELS else vector


def bits_of(labels):
    return [((labels >> b) & 1) == 1 for b in range(3)]


def sums_kernel(
    occ_hbm, vir_hbm, cd_hbm, t_hbm, v_hbm, keep, give, j_out, i_out,
    t_buf, v_buf, w_buf, total, occ, vir, cd, t_sem, v_sem, s_sem,
):
    rows, occupied, depth = t_buf.shape
    span = depth // V_CHUNKS
    small = [
        pltpu.make_async_copy(source, target, s_sem.at[n])
        for n, (source, target) in enumerate(((occ_hbm, occ), (vir_hbm, vir), (cd_hbm, cd)))
    ]
    v_copies = [
        pltpu.make_async_copy(
            v_hbm.at[pl.ds(c * span, span), :], v_buf.at[pl.ds(c * span, span), :], v_sem.at[c]
        )
        for c in range(V_CHUNKS)
    ]
    t_copy = pltpu.make_async_copy(t_hbm, t_buf, t_sem)
    for copy in (*small, *v_copies, t_copy):
        copy.start()
    pair, red = lax.axis_index("pair"), lax.axis_index("red")
    for copy in small:
        copy.wait()

    zero, one = jnp.zeros((), BF16), jnp.ones((), BF16)
    sublane = lax.broadcasted_iota(I32, (8, LANES), 0)
    lane_block = lax.broadcasted_iota(I32, (8, LANES), 1) // BLOCK

    def column(first):
        value = jnp.full((8, LANES), occ[first], I32)
        for s in range(1, 8):
            value = jnp.where(sublane == s, occ[first + s], value)
        return value

    occ_j = [column(8 * g) for g in range(occupied // 8)]
    occ_j16 = jnp.concatenate(occ_j, 0).astype(F32).astype(BF16)
    occ_i = [occ[pair * rows + i] for i in range(rows)]

    pieces = vir.shape[0] // LANES
    table = [
        jnp.broadcast_to(vir[pl.ds(LANES * n, LANES)].reshape(1, LANES), (8, LANES))
        for n in range(pieces)
    ]
    block_row = (lax.broadcasted_iota(I32, (LANES, LANES), 0) // BLOCK).astype(F32).astype(BF16)
    labels, masks = [], []
    for q in range(depth // LANES):
        index = cd[:, pl.ds(q * LANES, LANES)]
        index = jnp.concatenate([index, jnp.zeros((6, LANES), I32)], 0)
        within, piece = index % LANES, index // LANES
        found = jnp.take_along_axis(table[0], within, axis=1)
        for n in range(1, pieces):
            found = jnp.where(piece == n, jnp.take_along_axis(table[n], within, axis=1), found)
        label = found[0:1] ^ found[1:2]
        labels.append(label)
        spread = jnp.broadcast_to(label, (LANES, LANES)).astype(F32).astype(BF16)
        masks.append(jnp.where(spread == block_row, one, zero).T)

    for c in range(V_CHUNKS):
        v_copies[c].wait()
        for q in range(c * span // LANES, (c + 1) * span // LANES):
            ks = pl.ds(q * LANES, LANES)
            mask = masks[q] != zero
            folded = jnp.where(mask, v_buf[ks, 0:LANES], zero)
            for p in range(1, OWNERS):
                part = jnp.where(mask, v_buf[ks, pl.ds(p * LANES, LANES)], zero)
                folded = folded + turn(part, p)
            w_buf[ks, :] = folded

    t_copy.wait()
    masked = []
    for i in range(rows):
        row = []
        for q in range(depth // LANES):
            wanted = jnp.broadcast_to(labels[q] ^ occ_i[i], (occupied, LANES))
            wanted = wanted.astype(F32).astype(BF16)
            row.append(jnp.where(wanted == occ_j16, t_buf[i, :, pl.ds(q * LANES, LANES)], zero))
        masked.append(jnp.concatenate(row, 1))
    total[...] = jnp.dot(
        jnp.concatenate(masked, 0), w_buf[...], preferred_element_type=F32
    )

    lane_bits = bits_of(lane_block)
    occ_i_lane = jnp.zeros((8, LANES), I32)
    for i in range(rows):
        occ_i_lane = jnp.where(lane_block == i, occ_i[i], occ_i_lane)
    me = pair * REDS + red
    j_rows = occupied // REDS
    for g in range(occupied // 8):
        held = [turn(total[pl.ds(i * occupied + g * 8, 8), :], i) for i in range(rows)]
        skewed = pick(held, lane_bits)
        held = [turn(skewed[-d % 8], -d) for d in range(8)]
        held = pick(held, bits_of(occ_j[g] ^ occ_i_lane))
        for p in range(OWNERS):
            to = place((p * REDS + g * 8 // j_rows) ^ me)
            at = (to % 16, pl.ds(g * 8 % j_rows, 8), slice(None))

            @pl.when(to < 16)
            def _(p=p, at=at, held=held):
                keep[at] = held[p]

            @pl.when(to >= 16)
            def _(p=p, at=at, held=held):
                give[at] = held[p]

    for g in range(j_rows // 8):
        value = column(red * j_rows + 8 * g) ^ lane_block
        j_out[pl.ds(8 * g, 8), :] = value.astype(F32)
    for a in range(OWNERS):
        i_out[pl.ds(8 * a, 8), :] = column((pair ^ a) * rows).astype(F32)


def spread_kernel(held, came, j_in, i_in, out, buf, sem):
    pair = lax.axis_index("pair")
    lane_block = lax.broadcasted_iota(I32, (1, LANES), 1) // BLOCK
    bits = bits_of(jnp.broadcast_to(lane_block, held.shape[1:]))
    j_side = j_in[...].astype(BF16)
    copies = []
    for a in range(OWNERS):
        block = (held if a < 4 else came)[a % 4]
        level = [block]
        for b in (2, 1, 0):
            level = [
                jnp.where(bits[b], *((v, turn(v, -(2**b))) if upper else (turn(v, 2**b), v)))
                for v in level
                for upper in (False, True)
            ]
        for i in range(8):
            wanted = jnp.broadcast_to(i_in[pl.ds(8 * a + i, 1), :], j_side.shape).astype(BF16)
            buf[a, i] = jnp.where(wanted == j_side, level[i], jnp.zeros((), BF16))
        copy = pltpu.make_async_copy(buf.at[a], out.at[pl.ds((pair ^ a) * 8, 8)], sem.at[a])
        copy.start()
        copies.append(copy)
    for copy in copies:
        copy.wait()


def in_hbm(*arrays):
    return [pltpu.with_memory_space_constraint(a, pltpu.HBM) for a in arrays]


def fast(amplitudes, integrals, occ_irrep, vir_irrep, cd_orbitals, ab_orbitals):
    rows, occupied, depth = amplitudes.shape
    j_rows = occupied // REDS
    vmem, hbm = pl.BlockSpec(memory_space=pltpu.VMEM), pl.BlockSpec(memory_space=pltpu.HBM)
    half = jax.ShapeDtypeStruct((16, j_rows, LANES), F32)
    keep, give, j_side, i_side = pl.pallas_call(
        sums_kernel,
        out_shape=(
            half,
            half,
            jax.ShapeDtypeStruct((j_rows, LANES), F32),
            jax.ShapeDtypeStruct((occupied, LANES), F32),
        ),
        in_specs=[hbm] * 5,
        out_specs=(vmem,) * 4,
        scratch_shapes=[
            pltpu.VMEM(amplitudes.shape, BF16),
            pltpu.VMEM(integrals.shape, BF16),
            pltpu.VMEM((depth, LANES), BF16),
            pltpu.VMEM((rows * occupied, LANES), F32),
            pltpu.SMEM(occ_irrep.shape, I32),
            pltpu.VMEM(vir_irrep.shape, I32),
            pltpu.VMEM(cd_orbitals.shape, I32),
            pltpu.SemaphoreType.DMA,
            pltpu.SemaphoreType.DMA((V_CHUNKS,)),
            pltpu.SemaphoreType.DMA((3,)),
        ],
        compiler_params=pltpu.CompilerParams(vmem_limit_bytes=32 * 2**20),
        name="sums",
    )(*in_hbm(occ_irrep, vir_irrep, cd_orbitals, amplitudes, integrals))

    def swap(block, pattern):
        pairs = [(d, d ^ pattern) for d in range(OWNERS * REDS)]
        return lax.ppermute(block, ("pair", "red"), pairs)

    chip = keep + swap(give, 0b00001)
    done = (chip[:8] + swap(chip[8:], 0b00011)).astype(BF16)
    came = swap(done[4:], 0b00101)
    both = jnp.stack([done[:4], came]).reshape(2, 2, 2, j_rows, LANES)
    came = swap(both[:, 1], 0b01001)
    both = jnp.stack([both[:, 0], came]).reshape(4, 2, j_rows, LANES)
    held = both[:, 0]
    came = swap(both[:, 1], 0b10001)

    return pl.pallas_call(
        spread_kernel,
        out_shape=jax.ShapeDtypeStruct((occupied, j_rows, LANES), BF16),
        in_specs=[vmem] * 4,
        out_specs=hbm,
        scratch_shapes=[
            pltpu.VMEM((OWNERS, 8, j_rows, LANES), BF16),
            pltpu.SemaphoreType.DMA((OWNERS,)),
        ],
        name="spread",
    )(held, came, j_side, i_side)


def solution(mesh):
    def local(amplitudes, integrals, occ_irrep, vir_irrep, cd_orbitals, ab_orbitals):
        sizes = mesh.shape["pair"], mesh.shape["red"], amplitudes.shape[0], ab_orbitals.shape[1]
        form = fast if sizes == (OWNERS, REDS, 8, LANES) else general
        return form(amplitudes, integrals, occ_irrep, vir_irrep, cd_orbitals, ab_orbitals)

    in_specs = (P("pair", None, "red"), P("red", None), P(), P(), P(None, "red"), P(None, "pair"))
    out_specs = P(None, "red", "pair")
    return jax.shard_map(local, mesh=mesh, in_specs=in_specs, out_specs=out_specs, check_vma=False)
```

time: 135 us -> 26.1 us (0.19)
  blocking collectives: 55.4 us -> 0 us
  waiting for transfers between devices: 30.2 us -> 7.49 us
  local copies, waits for them, and re-layouts: 18.3 us -> 1.23 us
  between operations: 13.5 us -> 0.07 us
  other arithmetic: 12.5 us -> 0.04 us
  starting transfers between devices: 0.01 us -> 9.67 us
  Pallas kernels: 0 us -> 7.33 us
  matrix products: 5.21 us -> 0 us
    all_to_all x1 -> x0, blocking collectives: 55.4 us -> none  [local(): lax.all_to_all(partial_sums, 'pair', split_axis=2, concat_axis=0, tiled=T...]
    reduce_scatter x1 -> x0, waiting for transfers between devices: 30.2 us -> none  [local(): summed = lax.psum_scatter(moved, 'red', scatter_dimension=1, tiled=True)]
    ppermute x0 -> x5, starting transfers between devices: none -> 9.67 us  [swap(): return lax.ppermute(block, ('pair', 'red'), pairs)]
    unnamed x8 -> x6, local copies, waits for them, and re-layouts: 9.53 us -> 0.61 us
    ppermute x0 -> x5, waiting for transfers between devices: none -> 7.49 us  [swap(): return lax.ppermute(block, ('pair', 'red'), pairs)]
    pallas_call x0 -> x2, Pallas kernels: none -> 7.33 us  [the longest x1 5.5 us: fast(): pl.pallas_call(sums_kernel, out_shape=(half, half, jax.ShapeDtypeStruct((...]
    all_to_all x1 -> x0, other arithmetic: 7.22 us -> none  [local(): lax.all_to_all(partial_sums, 'pair', split_axis=2, concat_axis=0, tiled=T...]
    dot_general x1 -> x0, matrix products: 5.21 us -> none  [local(): jnp.dot(masked.reshape(own_rows * occupied, masked.shape[2]), integrals,...]
  transfers between devices with their start and end apart: 1 -> 5, of which waited for: 1 -> 5; matrix products, arithmetic and copies ran while one was open for 0% -> 0% of each run, Pallas kernels for 0% -> 0%
where the time goes in v1:
time: 26.1 us; the launch traced here: 25.8 us
  starting transfers between devices  9.67 us (37%)
  waiting for transfers between devices  7.49 us (29%)
  Pallas kernels  7.33 us (28%)
  local copies, waits for them, and re-layouts  1.23 us (5%)
    ppermute x5, starting transfers between devices, swap(): return lax.ppermute(block, ('pair', 'red'), pairs)  9.67 us
    ppermute x5, waiting for transfers between devices, swap(): return lax.ppermute(block, ('pair', 'red'), pairs)  7.49 us
    pallas_call x1, Pallas kernels, fast(): pl.pallas_call(sums_kernel, out_shape=(half, half, jax.ShapeDtypeStruct((...  5.5 us
    pallas_call x1, Pallas kernels, fast(): pl.pallas_call(spread_kernel, out_shape=jax.ShapeDtypeStruct((occupied, j...  1.83 us
    squeeze x1, local copies, waits for them, and re-layouts, fast(): came = swap(both[:, 1], 17)  0.61 us
    unnamed x6, local copies, waits for them, and re-layouts  0.61 us
  transfers between devices with their start and end apart: 5, of which 5 were waited for; matrix products, arithmetic and copies ran while one was open for 0% of the time, Pallas kernels for 0%

profile of v1, /device:TPU:0, one launch (start us, length us, event | category | flops | bytes accessed | tf_op | source)
XLA Modules:
  0.0 25.8 jit_solution(12365619129003216863)
XLA Ops:
  0.0 5.5 %sums.1 = (f32[16,16,128]{2,1,0:T(8,128)S(1)}, f32[16,16,128]{2,1,0:T(8,128)S(1)}, f32[16,128]{1,0:T(8,128)S(1)}, f32[64,128]{1,0:T(8,128)S(1)}) custom-call(s32[64]{0:T(128)} %occ_hbm.1, s32[512]{0:T(512)} %vir_hbm.1, s32[2,2048]{1,0:T(2,128)} %cd_hbm.1, bf16[8,64,2048]{2,1,0:T(8,128)(2,1)} %t_hbm.1, bf16[2048,1024]{1,0:T(8,128)(2,1)} %v_hbm.1), custom_call_target="tpu_custom_call" | custom-call | tf_op jit(solution)/shard_map/sums/pallas_call | solution.py:219
  5.5 0.0 copy-start
  5.5 0.0 copy-start.1
  5.5 0.5 %collective-permute-start = (f32[16,16,128]{2,1,0:T(8,128)S(1)}, f32[16,16,128]{2,1,0:T(8,128)S(1)}, u32[]{:S(2)}, u32[]{:S(2)}) collective-permute-start(f32[16,16,128]{2,1,0:T(8,128)S(1)} %get-tuple-element.10), channel_id=1, source_target_pairs={{0,1},{1,0},{2,3},{3,2},{4,5},{5,4},{6,7},{7,6},{8,9},{9,8},{10,11... | collective-permute-start | bytes 393224 | tf_op jit(solution)/shard_map/ppermute | solution.py:247
  6.0 1.0 %collective-permute-done = f32[16,16,128]{2,1,0:T(8,128)S(1)} collective-permute-done((f32[16,16,128]{2,1,0:T(8,128)S(1)}, f32[16,16,128]{2,1,0:T(8,128)S(1)}, u32[]{:S(2)}, u32[]{:S(2)}) %collective-permute-start) | collective-permute-done | bytes 131104 | tf_op jit(solution)/shard_map/ppermute | solution.py:247
  7.0 0.0 copy-done
  7.1 0.0 copy-done.1
  7.1 2.7 %collective-permute-start.1 = (f32[8,16,128]{2,1,0:T(8,128)S(1)}, f32[8,16,128]{2,1,0:T(8,128)S(1)}, u32[]{:S(2)}, u32[]{:S(2)}) collective-permute-start(f32[8,16,128]{2,1,0:T(8,128)S(1)} %slice.33), channel_id=1, source_target_pairs={{0,3},{1,2},{2,1},{3,0},{4,7},{5,6},{6,5},{7,4},{8,11},{9,10},{10,... | collective-permute-start | bytes 196616 | tf_op jit(solution)/shard_map/ppermute | solution.py:247
  9.7 2.2 %collective-permute-done.1 = f32[8,16,128]{2,1,0:T(8,128)S(1)} collective-permute-done((f32[8,16,128]{2,1,0:T(8,128)S(1)}, f32[8,16,128]{2,1,0:T(8,128)S(1)}, u32[]{:S(2)}, u32[]{:S(2)}) %collective-permute-start.1) | collective-permute-done | bytes 65568 | tf_op jit(solution)/shard_map/ppermute | solution.py:247
  12.0 2.0 %collective-permute-start.2 = (bf16[4,16,128]{2,1,0:T(8,128)(2,1)S(1)}, bf16[4,16,128]{2,1,0:T(8,128)(2,1)S(1)}, u32[]{:S(2)}, u32[]{:S(2)}) collective-permute-start(bf16[4,16,128]{2,1,0:T(8,128)(2,1)S(1)} %get-tuple-element.18), channel_id=1, source_target_pairs={{0,5},{1,4},{2,7},{3,6},{4,1},{5,0},{6,3},{7,2},{8,13},{9,12},{10,... | collective-permute-start | bytes 49160 | tf_op jit(solution)/shard_map/ppermute | solution.py:247
  13.9 1.4 %collective-permute-done.2 = bf16[4,16,128]{2,1,0:T(8,128)(2,1)S(1)} collective-permute-done((bf16[4,16,128]{2,1,0:T(8,128)(2,1)S(1)}, bf16[4,16,128]{2,1,0:T(8,128)(2,1)S(1)}, u32[]{:S(2)}, u32[]{:S(2)}) %collective-permute-start.2) | collective-permute-done | bytes 16416 | tf_op jit(solution)/shard_map/ppermute | solution.py:247
  15.4 1.8 %collective-permute-start.3 = (bf16[2,2,16,128]{3,2,0,1:T(8,128)(2,1)S(1)}, bf16[2,2,16,128]{3,2,0,1:T(8,128)(2,1)S(1)}, u32[]{:S(2)}, u32[]{:S(2)}) collective-permute-start(bf16[2,2,16,128]{3,2,0,1:T(8,128)(2,1)S(1)} %get-tuple-element.16), channel_id=1, source_target_pairs={{0,9},{1,8},{2,11},{3,10},{4,13},{5,12},{6,15},{7,14},{8,1},{9,0},... | collective-permute-start | bytes 49160 | tf_op jit(solution)/shard_map/ppermute | solution.py:247
  17.2 1.4 %collective-permute-done.3 = bf16[2,2,16,128]{3,2,0,1:T(8,128)(2,1)S(1)} collective-permute-done((bf16[2,2,16,128]{3,2,0,1:T(8,128)(2,1)S(1)}, bf16[2,2,16,128]{3,2,0,1:T(8,128)(2,1)S(1)}, u32[]{:S(2)}, u32[]{:S(2)}) %collective-permute-start.3) | collective-permute-done | bytes 16416 | tf_op jit(solution)/shard_map/ppermute | solution.py:247
  18.6 0.6 %slice_bitcast_fusion = (bf16[4,16,128]{2,1,0:T(8,128)(2,1)S(1)}, bf16[4,16,128]{2,1,0:T(8,128)(2,1)}) fusion(bf16[4,2,16,128]{3,2,0,1:T(8,128)(2,1)S(1)} %bitcast.18), kind=kLoop, calls=%fused_computation.7 | loop fusion | bytes 65536 | tf_op jit(solution)/shard_map/squeeze | solution.py:256
  19.2 2.7 %collective-permute-start.4 = (bf16[4,16,128]{2,1,0:T(8,128)(2,1)S(1)}, bf16[4,16,128]{2,1,0:T(8,128)(2,1)S(1)}, u32[]{:S(2)}, u32[]{:S(2)}) collective-permute-start(bf16[4,16,128]{2,1,0:T(8,128)(2,1)S(1)} %get-tuple-element.13), channel_id=1, source_target_pairs={{0,17},{1,16},{2,19},{3,18},{4,21},{5,20},{6,23},{7,22},{8,25},{9,... | collective-permute-start | bytes 49160 | tf_op jit(solution)/shard_map/ppermute | solution.py:247
  22.0 1.4 %collective-permute-done.4.came = bf16[4,16,128]{2,1,0:T(8,128)(2,1)S(1)} collective-permute-done((bf16[4,16,128]{2,1,0:T(8,128)(2,1)S(1)}, bf16[4,16,128]{2,1,0:T(8,128)(2,1)S(1)}, u32[]{:S(2)}, u32[]{:S(2)}) %collective-permute-start.4) | collective-permute-done | bytes 16416 | tf_op jit(solution)/shard_map/ppermute | solution.py:247
  23.4 0.0 copy-start.2
  23.4 0.6 %copy-done.2 = bf16[4,16,128]{2,1,0:T(8,128)(2,1)} copy-done((bf16[4,16,128]{2,1,0:T(8,128)(2,1)}, bf16[4,16,128]{2,1,0:T(8,128)(2,1)S(1)}, u32[]{:S(2)}) %copy-start.2) | copy-done | bytes 16408
  24.0 1.8 %spread.1 = bf16[64,16,128]{2,1,0:T(8,128)(2,1)} custom-call(bf16[4,16,128]{2,1,0:T(8,128)(2,1)} %get-tuple-element.14.held, bf16[4,16,128]{2,1,0:T(8,128)(2,1)} %copy-done.2, f32[16,128]{1,0:T(8,128)} %copy-done.1, f32[64,128]{1,0:T(8,128)} %copy-done), custom_call_target="tpu_custom_call" | custom-call | tf_op jit(solution)/shard_map/spread/pallas_call | solution.py:258
  (6 shorter events, 0.0 us)
Async XLA Ops:
  5.5 1.5 %copy-start = (f32[64,128]{1,0:T(8,128)}, f32[64,128]{1,0:T(8,128)S(1)}, u32[]{:S(2)}) copy-start(f32[64,128]{1,0:T(8,128)S(1)} %get-tuple-element.12.i_in) | copy-start | bytes 98308
  5.5 1.6 %copy-start.1 = (f32[16,128]{1,0:T(8,128)}, f32[16,128]{1,0:T(8,128)S(1)}, u32[]{:S(2)}) copy-start(f32[16,128]{1,0:T(8,128)S(1)} %get-tuple-element.11.j_in) | copy-start | bytes 24580
  5.5 1.5 %collective-permute-start = (f32[16,16,128]{2,1,0:T(8,128)S(1)}, f32[16,16,128]{2,1,0:T(8,128)S(1)}, u32[]{:S(2)}, u32[]{:S(2)}) collective-permute-start(f32[16,16,128]{2,1,0:T(8,128)S(1)} %get-tuple-element.10), channel_id=1, source_target_pairs={{0,1},{1,0},{2,3},{3,2},{4,5},{5,4},{6,7},{7,6},{8,9},{9,8},{10,11... | collective-permute-start | bytes 393224 | tf_op jit(solution)/shard_map/ppermute | solution.py:247
  7.1 4.8 %collective-permute-start.1 = (f32[8,16,128]{2,1,0:T(8,128)S(1)}, f32[8,16,128]{2,1,0:T(8,128)S(1)}, u32[]{:S(2)}, u32[]{:S(2)}) collective-permute-start(f32[8,16,128]{2,1,0:T(8,128)S(1)} %slice.33), channel_id=1, source_target_pairs={{0,3},{1,2},{2,1},{3,0},{4,7},{5,6},{6,5},{7,4},{8,11},{9,10},{10,... | collective-permute-start | bytes 196616 | tf_op jit(solution)/shard_map/ppermute | solution.py:247
  12.0 3.4 %collective-permute-start.2 = (bf16[4,16,128]{2,1,0:T(8,128)(2,1)S(1)}, bf16[4,16,128]{2,1,0:T(8,128)(2,1)S(1)}, u32[]{:S(2)}, u32[]{:S(2)}) collective-permute-start(bf16[4,16,128]{2,1,0:T(8,128)(2,1)S(1)} %get-tuple-element.18), channel_id=1, source_target_pairs={{0,5},{1,4},{2,7},{3,6},{4,1},{5,0},{6,3},{7,2},{8,13},{9,12},{10,... | collective-permute-start | bytes 49160 | tf_op jit(solution)/shard_map/ppermute | solution.py:247
  15.4 3.2 %collective-permute-start.3 = (bf16[2,2,16,128]{3,2,0,1:T(8,128)(2,1)S(1)}, bf16[2,2,16,128]{3,2,0,1:T(8,128)(2,1)S(1)}, u32[]{:S(2)}, u32[]{:S(2)}) collective-permute-start(bf16[2,2,16,128]{3,2,0,1:T(8,128)(2,1)S(1)} %get-tuple-element.16), channel_id=1, source_target_pairs={{0,9},{1,8},{2,11},{3,10},{4,13},{5,12},{6,15},{7,14},{8,1},{9,0},... | collective-permute-start | bytes 49160 | tf_op jit(solution)/shard_map/ppermute | solution.py:247
  19.2 4.2 %collective-permute-start.4 = (bf16[4,16,128]{2,1,0:T(8,128)(2,1)S(1)}, bf16[4,16,128]{2,1,0:T(8,128)(2,1)S(1)}, u32[]{:S(2)}, u32[]{:S(2)}) collective-permute-start(bf16[4,16,128]{2,1,0:T(8,128)(2,1)S(1)} %get-tuple-element.13), channel_id=1, source_target_pairs={{0,17},{1,16},{2,19},{3,18},{4,21},{5,20},{6,23},{7,22},{8,25},{9,... | collective-permute-start | bytes 49160 | tf_op jit(solution)/shard_map/ppermute | solution.py:247
  23.4 0.6 %copy-start.2 = (bf16[4,16,128]{2,1,0:T(8,128)(2,1)}, bf16[4,16,128]{2,1,0:T(8,128)(2,1)S(1)}, u32[]{:S(2)}) copy-start(bf16[4,16,128]{2,1,0:T(8,128)(2,1)S(1)} %collective-permute-done.4.came) | copy-start | bytes 49156

commit v2 on v1

--- a/solution.py
+++ b/solution.py
@@ -73,7 +73,7 @@
 
 
 def sums_kernel(
-    occ_hbm, vir_hbm, cd_hbm, t_hbm, v_hbm, keep, give, j_out, i_out,
+    occ_hbm, vir_hbm, cd_hbm, t_hbm, v_hbm, sums, j_out, i_out,
     t_buf, v_buf, w_buf, total, occ, vir, cd, t_sem, v_sem, s_sem,
 ):
     rows, occupied, depth = t_buf.shape
@@ -109,6 +109,13 @@
     occ_j16 = jnp.concatenate(occ_j, 0).astype(F32).astype(BF16)
     occ_i = [occ[pair * rows + i] for i in range(rows)]
 
+    j_rows = occupied // REDS
+    for g in range(j_rows // 8):
+        value = column(red * j_rows + 8 * g) ^ lane_block
+        j_out[pl.ds(8 * g, 8), :] = value.astype(F32)
+    for a in range(OWNERS):
+        i_out[pl.ds(8 * a, 8), :] = column((pair ^ a) * rows).astype(F32)
+
     pieces = vir.shape[0] // LANES
     table = [
         jnp.broadcast_to(vir[pl.ds(LANES * n, LANES)].reshape(1, LANES), (8, LANES))
@@ -157,7 +164,6 @@
     for i in range(rows):
         occ_i_lane = jnp.where(lane_block == i, occ_i[i], occ_i_lane)
     me = pair * REDS + red
-    j_rows = occupied // REDS
     for g in range(occupied // 8):
         held = [turn(total[pl.ds(i * occupied + g * 8, 8), :], i) for i in range(rows)]
         skewed = pick(held, lane_bits)
@@ -165,32 +171,19 @@
         held = pick(held, bits_of(occ_j[g] ^ occ_i_lane))
         for p in range(OWNERS):
             to = place((p * REDS + g * 8 // j_rows) ^ me)
-            at = (to % 16, pl.ds(g * 8 % j_rows, 8), slice(None))
-
-            @pl.when(to < 16)
-            def _(p=p, at=at, held=held):
-                keep[at] = held[p]
-
-            @pl.when(to >= 16)
-            def _(p=p, at=at, held=held):
-                give[at] = held[p]
-
-    for g in range(j_rows // 8):
-        value = column(red * j_rows + 8 * g) ^ lane_block
-        j_out[pl.ds(8 * g, 8), :] = value.astype(F32)
-    for a in range(OWNERS):
-        i_out[pl.ds(8 * a, 8), :] = column((pair ^ a) * rows).astype(F32)
-
-
-def spread_kernel(held, came, j_in, i_in, out, buf, sem):
+            sums[to, pl.ds(g * 8 % j_rows, 8), :] = held[p]
+
+
+def spread_kernel(first, blocks, j_in, i_in, *refs):
+    out, buf, sem = refs[-3:]
     pair = lax.axis_index("pair")
-    lane_block = lax.broadcasted_iota(I32, (1, LANES), 1) // BLOCK
-    bits = bits_of(jnp.broadcast_to(lane_block, held.shape[1:]))
+    lane_block = lax.broadcasted_iota(I32, blocks.shape[1:], 1) // BLOCK
+    bits = bits_of(lane_block)
     j_side = j_in[...].astype(BF16)
     copies = []
-    for a in range(OWNERS):
-        block = (held if a < 4 else came)[a % 4]
-        level = [block]
+    for n in range(4):
+        a = first + n
+        level = [blocks[n]]
         for b in (2, 1, 0):
             level = [
                 jnp.where(bits[b], *((v, turn(v, -(2**b))) if upper else (turn(v, 2**b), v)))
@@ -199,14 +192,35 @@
             ]
         for i in range(8):
             wanted = jnp.broadcast_to(i_in[pl.ds(8 * a + i, 1), :], j_side.shape).astype(BF16)
-            buf[a, i] = jnp.where(wanted == j_side, level[i], jnp.zeros((), BF16))
-        copy = pltpu.make_async_copy(buf.at[a], out.at[pl.ds((pair ^ a) * 8, 8)], sem.at[a])
+            buf[n, i] = jnp.where(wanted == j_side, level[i], jnp.zeros((), BF16))
+        copy = pltpu.make_async_copy(buf.at[n], out.at[pl.ds((pair ^ a) * 8, 8)], sem.at[n])
         copy.start()
         copies.append(copy)
     for copy in copies:
         copy.wait()
 
 
+def spread(first, blocks, j_side, i_side, *so_far):
+    occupied, j_rows = i_side.shape[0], j_side.shape[0]
+    vmem, hbm = pl.BlockSpec(memory_space=pltpu.VMEM), pl.BlockSpec(memory_space=pltpu.HBM)
+    return pl.pallas_call(
+        functools.partial(spread_kernel, first),
+        out_shape=jax.ShapeDtypeStruct((occupied, j_rows, LANES), BF16),
+        in_specs=[vmem] * 3 + [hbm] * len(so_far),
+        out_specs=hbm,
+        scratch_shapes=[
+            pltpu.VMEM((4, 8, j_rows, LANES), BF16),
+            pltpu.SemaphoreType.DMA((4,)),
+        ],
+        input_output_aliases={3: 0} if so_far else {},
+        compiler_params=pltpu.CompilerParams(vmem_limit_bytes=8 * 2**20),
+        cost_estimate=pl.CostEstimate(
+            flops=2 * 10**6, bytes_accessed=2 * occupied * j_rows * LANES, transcendentals=0
+        ),
+        name="spread",
+    )(blocks, j_side, i_side, *so_far)
+
+
 def in_hbm(*arrays):
     return [pltpu.with_memory_space_constraint(a, pltpu.HBM) for a in arrays]
 
@@ -215,17 +229,15 @@
     rows, occupied, depth = amplitudes.shape
     j_rows = occupied // REDS
     vmem, hbm = pl.BlockSpec(memory_space=pltpu.VMEM), pl.BlockSpec(memory_space=pltpu.HBM)
-    half = jax.ShapeDtypeStruct((16, j_rows, LANES), F32)
-    keep, give, j_side, i_side = pl.pallas_call(
+    sums, j_side, i_side = pl.pallas_call(
         sums_kernel,
         out_shape=(
-            half,
-            half,
+            jax.ShapeDtypeStruct((OWNERS * REDS, j_rows, LANES), F32),
             jax.ShapeDtypeStruct((j_rows, LANES), F32),
             jax.ShapeDtypeStruct((occupied, LANES), F32),
         ),
         in_specs=[hbm] * 5,
-        out_specs=(vmem,) * 4,
+        out_specs=(vmem,) * 3,
         scratch_shapes=[
             pltpu.VMEM(amplitudes.shape, BF16),
             pltpu.VMEM(integrals.shape, BF16),
@@ -246,7 +258,7 @@
         pairs = [(d, d ^ pattern) for d in range(OWNERS * REDS)]
         return lax.ppermute(block, ("pair", "red"), pairs)
 
-    chip = keep + swap(give, 0b00001)
+    chip = sums[:16] + swap(sums[16:], 0b00001)
     done = (chip[:8] + swap(chip[8:], 0b00011)).astype(BF16)
     came = swap(done[4:], 0b00101)
     both = jnp.stack([done[:4], came]).reshape(2, 2, 2, j_rows, LANES)
@@ -255,17 +267,8 @@
     held = both[:, 0]
     came = swap(both[:, 1], 0b10001)
 
-    return pl.pallas_call(
-        spread_kernel,
-        out_shape=jax.ShapeDtypeStruct((occupied, j_rows, LANES), BF16),
-        in_specs=[vmem] * 4,
-        out_specs=hbm,
-        scratch_shapes=[
-            pltpu.VMEM((OWNERS, 8, j_rows, LANES), BF16),
-            pltpu.SemaphoreType.DMA((OWNERS,)),
-        ],
-        name="spread",
-    )(held, came, j_side, i_side)
+    half = spread(0, held, j_side, i_side)
+    return spread(4, came, j_side, i_side, half)
 
 
 def solution(mesh):

time: 26.1 us -> 22.6 us (0.87)
  Pallas kernels: 7.33 us -> 6.03 us
  local copies, waits for them, and re-layouts: 1.23 us -> 0.03 us
  waiting for transfers between devices: 7.49 us -> 6.57 us
    pallas_call x2 -> x3, Pallas kernels: 7.33 us -> 6.03 us  [the longest x1 4.2 us: fast(): pl.pallas_call(sums_kernel, out_shape=(jax.ShapeDtypeStruct((OWNERS * RED...]
    ppermute x5, waiting for transfers between devices: 7.49 us -> 6.57 us  [swap(): return lax.ppermute(block, ('pair', 'red'), pairs)]
    unnamed x6 -> x0, local copies, waits for them, and re-layouts: 0.61 us -> none
    squeeze x1, local copies, waits for them, and re-layouts: 0.61 us -> 0.01 us  [fast(): held = both[:, 0]]
  transfers between devices with their start and end apart: 5 -> 5, of which waited for: 5 -> 5; matrix products, arithmetic and copies ran while one was open for 0% -> 0% of each run, Pallas kernels for 0% -> 4%
where the time goes in v2:
time: 22.6 us; the launch traced here: 22.5 us
  starting transfers between devices  9.75 us (43%)
  waiting for transfers between devices  6.57 us (29%)
  Pallas kernels  6.03 us (27%)
    ppermute x5, starting transfers between devices, swap(): return lax.ppermute(block, ('pair', 'red'), pairs)  9.75 us
    ppermute x5, waiting for transfers between devices, swap(): return lax.ppermute(block, ('pair', 'red'), pairs)  6.57 us
    pallas_call x1, Pallas kernels, fast(): pl.pallas_call(sums_kernel, out_shape=(jax.ShapeDtypeStruct((OWNERS * RED...  4.2 us
    pallas_call x2, Pallas kernels, spread(): pl.pallas_call(functools.partial(spread_kernel, first), out_shape=jax.Sha...  1.83 us
  transfers between devices with their start and end apart: 5, of which 5 were waited for; matrix products, arithmetic and copies ran while one was open for 0% of the time, Pallas kernels for 4%

profile of v2, /device:TPU:0, one launch (start us, length us, event | category | flops | bytes accessed | tf_op | source)
XLA Modules:
  0.0 22.5 jit_solution(3598446162876451704)
XLA Ops:
  0.0 4.2 %sums.1 = (f32[32,16,128]{2,1,0:T(8,128)S(1)}, f32[16,128]{1,0:T(8,128)S(1)}, f32[64,128]{1,0:T(8,128)S(1)}) custom-call(s32[64]{0:T(128)} %occ_hbm.1, s32[512]{0:T(512)} %vir_hbm.1, s32[2,2048]{1,0:T(2,128)} %cd_hbm.1, bf16[8,64,2048]{2,1,0:T(8,128)(2,1)} %t_hbm.1, bf16[2048,1024]{1,0:T(8,128)(2,1)} %v_hbm.1), custom_call_target="tpu_custom_call" | custom-call | tf_op jit(solution)/shard_map/sums/pallas_call | solution.py:232
  4.2 0.5 %collective-permute-start = (f32[16,16,128]{2,1,0:T(8,128)S(1)}, f32[16,16,128]{2,1,0:T(8,128)S(1)}, u32[]{:S(2)}, u32[]{:S(2)}) collective-permute-start(f32[16,16,128]{2,1,0:T(8,128)S(1)} %slice.31), channel_id=1, source_target_pairs={{0,1},{1,0},{2,3},{3,2},{4,5},{5,4},{6,7},{7,6},{8,9},{9,8},{10,11... | collective-permute-start | bytes 393224 | tf_op jit(solution)/shard_map/ppermute | solution.py:259
  4.8 1.0 %collective-permute-done = f32[16,16,128]{2,1,0:T(8,128)S(1)} collective-permute-done((f32[16,16,128]{2,1,0:T(8,128)S(1)}, f32[16,16,128]{2,1,0:T(8,128)S(1)}, u32[]{:S(2)}, u32[]{:S(2)}) %collective-permute-start) | collective-permute-done | bytes 131104 | tf_op jit(solution)/shard_map/ppermute | solution.py:259
  5.8 2.7 %collective-permute-start.1 = (f32[8,16,128]{2,1,0:T(8,128)S(1)}, f32[8,16,128]{2,1,0:T(8,128)S(1)}, u32[]{:S(2)}, u32[]{:S(2)}) collective-permute-start(f32[8,16,128]{2,1,0:T(8,128)S(1)} %slice.41), channel_id=1, source_target_pairs={{0,3},{1,2},{2,1},{3,0},{4,7},{5,6},{6,5},{7,4},{8,11},{9,10},{10,... | collective-permute-start | bytes 196616 | tf_op jit(solution)/shard_map/ppermute | solution.py:259
  8.4 2.2 %collective-permute-done.1 = f32[8,16,128]{2,1,0:T(8,128)S(1)} collective-permute-done((f32[8,16,128]{2,1,0:T(8,128)S(1)}, f32[8,16,128]{2,1,0:T(8,128)S(1)}, u32[]{:S(2)}, u32[]{:S(2)}) %collective-permute-start.1) | collective-permute-done | bytes 65568 | tf_op jit(solution)/shard_map/ppermute | solution.py:259
  10.6 2.0 %collective-permute-start.2 = (bf16[4,16,128]{2,1,0:T(8,128)(2,1)S(1)}, bf16[4,16,128]{2,1,0:T(8,128)(2,1)S(1)}, u32[]{:S(2)}, u32[]{:S(2)}) collective-permute-start(bf16[4,16,128]{2,1,0:T(8,128)(2,1)S(1)} %get-tuple-element.16), channel_id=1, source_target_pairs={{0,5},{1,4},{2,7},{3,6},{4,1},{5,0},{6,3},{7,2},{8,13},{9,12},{10,... | collective-permute-start | bytes 49160 | tf_op jit(solution)/shard_map/ppermute | solution.py:259
  12.6 1.4 %collective-permute-done.2 = bf16[4,16,128]{2,1,0:T(8,128)(2,1)S(1)} collective-permute-done((bf16[4,16,128]{2,1,0:T(8,128)(2,1)S(1)}, bf16[4,16,128]{2,1,0:T(8,128)(2,1)S(1)}, u32[]{:S(2)}, u32[]{:S(2)}) %collective-permute-start.2) | collective-permute-done | bytes 16416 | tf_op jit(solution)/shard_map/ppermute | solution.py:259
  14.1 1.8 %collective-permute-start.3 = (bf16[2,2,16,128]{3,2,0,1:T(8,128)(2,1)S(1)}, bf16[2,2,16,128]{3,2,0,1:T(8,128)(2,1)S(1)}, u32[]{:S(2)}, u32[]{:S(2)}) collective-permute-start(bf16[2,2,16,128]{3,2,0,1:T(8,128)(2,1)S(1)} %get-tuple-element.14), channel_id=1, source_target_pairs={{0,9},{1,8},{2,11},{3,10},{4,13},{5,12},{6,15},{7,14},{8,1},{9,0},... | collective-permute-start | bytes 49160 | tf_op jit(solution)/shard_map/ppermute | solution.py:259
  15.9 1.4 %collective-permute-done.3 = bf16[2,2,16,128]{3,2,0,1:T(8,128)(2,1)S(1)} collective-permute-done((bf16[2,2,16,128]{3,2,0,1:T(8,128)(2,1)S(1)}, bf16[2,2,16,128]{3,2,0,1:T(8,128)(2,1)S(1)}, u32[]{:S(2)}, u32[]{:S(2)}) %collective-permute-start.3) | collective-permute-done | bytes 16416 | tf_op jit(solution)/shard_map/ppermute | solution.py:259
  17.3 2.8 %collective-permute-start.4 = (bf16[4,16,128]{2,1,0:T(8,128)(2,1)S(1)}, bf16[4,16,128]{2,1,0:T(8,128)(2,1)S(1)}, u32[]{:S(2)}, u32[]{:S(2)}) collective-permute-start(bf16[4,16,128]{2,1,0:T(8,128)(2,1)S(1)} %get-tuple-element.12), channel_id=1, source_target_pairs={{0,17},{1,16},{2,19},{3,18},{4,21},{5,20},{6,23},{7,22},{8,25},{9,... | collective-permute-start | bytes 49160 | tf_op jit(solution)/shard_map/ppermute | solution.py:259
  20.1 0.9 %spread.2.refs_0_ = bf16[64,16,128]{2,1,0:T(8,128)(2,1)} custom-call(bf16[4,16,128]{2,1,0:T(8,128)(2,1)S(1)} %get-tuple-element.11.blocks, f32[16,128]{1,0:T(8,128)S(1)} %get-tuple-element.9.j_in, f32[64,128]{1,0:T(8,128)S(1)} %get-tuple-element.10.i_in), custom_call_target="tpu_custom_call" | custom-call | flops 2000000 | bytes 262144 | tf_op jit(solution)/shard_map/spread/pallas_call | solution.py:206
  21.0 0.5 %collective-permute-done.4.blocks = bf16[4,16,128]{2,1,0:T(8,128)(2,1)S(1)} collective-permute-done((bf16[4,16,128]{2,1,0:T(8,128)(2,1)S(1)}, bf16[4,16,128]{2,1,0:T(8,128)(2,1)S(1)}, u32[]{:S(2)}, u32[]{:S(2)}) %collective-permute-start.4) | collective-permute-done | bytes 16416 | tf_op jit(solution)/shard_map/ppermute | solution.py:259
  21.6 0.9 %spread.3 = bf16[64,16,128]{2,1,0:T(8,128)(2,1)} custom-call(bf16[4,16,128]{2,1,0:T(8,128)(2,1)S(1)} %collective-permute-done.4.blocks, f32[16,128]{1,0:T(8,128)S(1)} %get-tuple-element.9.j_in, f32[64,128]{1,0:T(8,128)S(1)} %get-tuple-element.10.i_in, bf16[64,16,128]{2,1,0:T(8,128)(2,1)} %spread.2.refs_0_), custom_call_target="tpu_custom_call", output_to_operand_aliasing={{}: (3, {})} | custom-call | flops 2000000 | bytes 262144 | tf_op jit(solution)/shard_map/spread/pallas_call | solution.py:206
  (8 shorter events, 0.1 us)
Async XLA Ops:
  4.2 1.5 %collective-permute-start = (f32[16,16,128]{2,1,0:T(8,128)S(1)}, f32[16,16,128]{2,1,0:T(8,128)S(1)}, u32[]{:S(2)}, u32[]{:S(2)}) collective-permute-start(f32[16,16,128]{2,1,0:T(8,128)S(1)} %slice.31), channel_id=1, source_target_pairs={{0,1},{1,0},{2,3},{3,2},{4,5},{5,4},{6,7},{7,6},{8,9},{9,8},{10,11... | collective-permute-start | bytes 393224 | tf_op jit(solution)/shard_map/ppermute | solution.py:259
  5.8 4.8 %collective-permute-start.1 = (f32[8,16,128]{2,1,0:T(8,128)S(1)}, f32[8,16,128]{2,1,0:T(8,128)S(1)}, u32[]{:S(2)}, u32[]{:S(2)}) collective-permute-start(f32[8,16,128]{2,1,0:T(8,128)S(1)} %slice.41), channel_id=1, source_target_pairs={{0,3},{1,2},{2,1},{3,0},{4,7},{5,6},{6,5},{7,4},{8,11},{9,10},{10,... | collective-permute-start | bytes 196616 | tf_op jit(solution)/shard_map/ppermute | solution.py:259
  10.6 3.4 %collective-permute-start.2 = (bf16[4,16,128]{2,1,0:T(8,128)(2,1)S(1)}, bf16[4,16,128]{2,1,0:T(8,128)(2,1)S(1)}, u32[]{:S(2)}, u32[]{:S(2)}) collective-permute-start(bf16[4,16,128]{2,1,0:T(8,128)(2,1)S(1)} %get-tuple-element.16), channel_id=1, source_target_pairs={{0,5},{1,4},{2,7},{3,6},{4,1},{5,0},{6,3},{7,2},{8,13},{9,12},{10,... | collective-permute-start | bytes 49160 | tf_op jit(solution)/shard_map/ppermute | solution.py:259
  14.1 3.2 %collective-permute-start.3 = (bf16[2,2,16,128]{3,2,0,1:T(8,128)(2,1)S(1)}, bf16[2,2,16,128]{3,2,0,1:T(8,128)(2,1)S(1)}, u32[]{:S(2)}, u32[]{:S(2)}) collective-permute-start(bf16[2,2,16,128]{3,2,0,1:T(8,128)(2,1)S(1)} %get-tuple-element.14), channel_id=1, source_target_pairs={{0,9},{1,8},{2,11},{3,10},{4,13},{5,12},{6,15},{7,14},{8,1},{9,0},... | collective-permute-start | bytes 49160 | tf_op jit(solution)/shard_map/ppermute | solution.py:259
  17.3 4.2 %collective-permute-start.4 = (bf16[4,16,128]{2,1,0:T(8,128)(2,1)S(1)}, bf16[4,16,128]{2,1,0:T(8,128)(2,1)S(1)}, u32[]{:S(2)}, u32[]{:S(2)}) collective-permute-start(bf16[4,16,128]{2,1,0:T(8,128)(2,1)S(1)} %get-tuple-element.12), channel_id=1, source_target_pairs={{0,17},{1,16},{2,19},{3,18},{4,21},{5,20},{6,23},{7,22},{8,25},{9,... | collective-permute-start | bytes 49160 | tf_op jit(solution)/shard_map/ppermute | solution.py:259

commit v3 on v2

--- a/solution.py
+++ b/solution.py
@@ -51,9 +51,11 @@
 
 
 def place(offset):
-    bit = [(offset >> b) & 1 for b in range(5)]
-    odd = bit[0] ^ bit[1] ^ bit[2] ^ bit[3] ^ bit[4]
-    return (((odd * 2 + bit[1]) * 2 + bit[2]) * 2 + bit[3]) * 2 + bit[4]
+    core, x, y, low, high = [(offset >> b) & 1 for b in range(5)]
+    return ((((core ^ y ^ low ^ high) * 2 + x) * 2 + low) * 2 + y) * 2 + high
+
+
+CORE, X, Y, LOW, HIGH = 0b00001, 0b00010, 0b00101, 0b01001, 0b10001
 
 
 def pick(vectors, shift_bits):
@@ -174,16 +176,15 @@
             sums[to, pl.ds(g * 8 % j_rows, 8), :] = held[p]
 
 
-def spread_kernel(first, blocks, j_in, i_in, *refs):
-    out, buf, sem = refs[-3:]
+def spread_kernel(offsets, j_in, i_in, *refs):
+    arrays, (out, buf, sem) = refs[: len(offsets)], refs[-3:]
     pair = lax.axis_index("pair")
-    lane_block = lax.broadcasted_iota(I32, blocks.shape[1:], 1) // BLOCK
-    bits = bits_of(lane_block)
     j_side = j_in[...].astype(BF16)
+    bits = bits_of(lax.broadcasted_iota(I32, j_side.shape, 1) // BLOCK)
+    sources = [(ref, k, a) for ref, of in zip(arrays, offsets) for k, a in enumerate(of)]
     copies = []
-    for n in range(4):
-        a = first + n
-        level = [blocks[n]]
+    for n, (ref, k, a) in enumerate(sources):
+        level = [ref[k]]
         for b in (2, 1, 0):
             level = [
                 jnp.where(bits[b], *((v, turn(v, -(2**b))) if upper else (turn(v, 2**b), v)))
@@ -200,25 +201,28 @@
         copy.wait()
 
 
-def spread(first, blocks, j_side, i_side, *so_far):
+def spread(j_side, i_side, blocks, so_far=None):
+    offsets, arrays = [of for of, _ in blocks], [array for _, array in blocks]
+    count = sum(len(of) for of in offsets)
     occupied, j_rows = i_side.shape[0], j_side.shape[0]
     vmem, hbm = pl.BlockSpec(memory_space=pltpu.VMEM), pl.BlockSpec(memory_space=pltpu.HBM)
+    earlier = [] if so_far is None else [so_far]
     return pl.pallas_call(
-        functools.partial(spread_kernel, first),
+        functools.partial(spread_kernel, offsets),
         out_shape=jax.ShapeDtypeStruct((occupied, j_rows, LANES), BF16),
-        in_specs=[vmem] * 3 + [hbm] * len(so_far),
+        in_specs=[vmem] * (2 + len(arrays)) + [hbm] * len(earlier),
         out_specs=hbm,
         scratch_shapes=[
-            pltpu.VMEM((4, 8, j_rows, LANES), BF16),
-            pltpu.SemaphoreType.DMA((4,)),
+            pltpu.VMEM((count, 8, j_rows, LANES), BF16),
+            pltpu.SemaphoreType.DMA((count,)),
         ],
-        input_output_aliases={3: 0} if so_far else {},
+        input_output_aliases={2 + len(arrays): 0} if earlier else {},
         compiler_params=pltpu.CompilerParams(vmem_limit_bytes=8 * 2**20),
         cost_estimate=pl.CostEstimate(
-            flops=2 * 10**6, bytes_accessed=2 * occupied * j_rows * LANES, transcendentals=0
+            flops=10**6, bytes_accessed=2 * count * 8 * j_rows * LANES, transcendentals=0
         ),
         name="spread",
-    )(blocks, j_side, i_side, *so_far)
+    )(j_side, i_side, *arrays, *earlier)
 
 
 def in_hbm(*arrays):
@@ -258,17 +262,17 @@
         pairs = [(d, d ^ pattern) for d in range(OWNERS * REDS)]
         return lax.ppermute(block, ("pair", "red"), pairs)
 
-    chip = sums[:16] + swap(sums[16:], 0b00001)
-    done = (chip[:8] + swap(chip[8:], 0b00011)).astype(BF16)
-    came = swap(done[4:], 0b00101)
-    both = jnp.stack([done[:4], came]).reshape(2, 2, 2, j_rows, LANES)
-    came = swap(both[:, 1], 0b01001)
-    both = jnp.stack([both[:, 0], came]).reshape(4, 2, j_rows, LANES)
-    held = both[:, 0]
-    came = swap(both[:, 1], 0b10001)
-
-    half = spread(0, held, j_side, i_side)
-    return spread(4, came, j_side, i_side, half)
+    shape = (2, 2, 2, 2, 2, j_rows, LANES)
+    sums = sums.reshape(shape)
+    chip = sums[0] + swap(sums[1], CORE)
+    low = swap(chip[0, 1], LOW)
+    across = swap(chip[1, 0], X)
+    corner = swap(chip[1, 1], X ^ LOW)
+    done = jnp.stack([(chip[0, 0] + across).astype(BF16), (low + corner).astype(BF16)])
+    both = jnp.stack([done[:, 0], swap(done[:, 1], Y)]).reshape(4, 2, j_rows, LANES)
+    high = swap(both[:, 1], HIGH)
+    out = spread(j_side, i_side, [((0, 2, 1, 3), both[:, 0])])
+    return spread(j_side, i_side, [((4, 6, 5, 7), high)], out)
 
 
 def solution(mesh):

time: 22.6 us -> 21.7 us (0.960)
  starting transfers between devices: 9.75 us -> 9.07 us
    ppermute x5 -> x6, starting transfers between devices: 9.75 us -> 9.07 us  [swap(): return lax.ppermute(block, ('pair', 'red'), pairs)]
    ppermute x5 -> x6, waiting for transfers between devices: 6.57 us -> 6.36 us  [swap(): return lax.ppermute(block, ('pair', 'red'), pairs)]
  transfers between devices with their start and end apart: 5 -> 6, of which waited for: 5 -> 5; matrix products, arithmetic and copies ran while one was open for 0% -> 0% of each run, Pallas kernels for 4% -> 4%
where the time goes in v3:
time: 21.7 us; the launch traced here: 21.6 us
  starting transfers between devices  9.07 us (42%)
  waiting for transfers between devices  6.36 us (29%)
  Pallas kernels  6.01 us (28%)
    ppermute x6, starting transfers between devices, swap(): return lax.ppermute(block, ('pair', 'red'), pairs)  9.07 us
    ppermute x6, waiting for transfers between devices, swap(): return lax.ppermute(block, ('pair', 'red'), pairs)  6.36 us
    pallas_call x1, Pallas kernels, fast(): pl.pallas_call(sums_kernel, out_shape=(jax.ShapeDtypeStruct((OWNERS * RED...  4.18 us
    pallas_call x2, Pallas kernels, spread(): pl.pallas_call(functools.partial(spread_kernel, offsets), out_shape=jax.S...  1.83 us
  transfers between devices with their start and end apart: 6, of which 5 were waited for; matrix products, arithmetic and copies ran while one was open for 0% of the time, Pallas kernels for 4%

profile of v3, /device:TPU:0, one launch (start us, length us, event | category | flops | bytes accessed | tf_op | source)
XLA Modules:
  0.0 21.6 jit_solution(13134481017756546963)
XLA Ops:
  0.0 4.2 %sums.1 = (f32[32,16,128]{2,1,0:T(8,128)S(1)}, f32[16,128]{1,0:T(8,128)S(1)}, f32[64,128]{1,0:T(8,128)S(1)}) custom-call(s32[64]{0:T(128)} %occ_hbm.1, s32[512]{0:T(512)} %vir_hbm.1, s32[2,2048]{1,0:T(2,128)} %cd_hbm.1, bf16[8,64,2048]{2,1,0:T(8,128)(2,1)} %t_hbm.1, bf16[2048,1024]{1,0:T(8,128)(2,1)} %v_hbm.1), custom_call_target="tpu_custom_call" | custom-call | tf_op jit(solution)/shard_map/sums/pallas_call | solution.py:236
  4.2 0.5 %collective-permute-start = (f32[2,2,2,2,16,128]{5,4,3,2,1,0:T(8,128)S(1)}, f32[2,2,2,2,16,128]{5,4,3,2,1,0:T(8,128)S(1)}, u32[]{:S(2)}, u32[]{:S(2)}) collective-permute-start(f32[2,2,2,2,16,128]{5,4,3,2,1,0:T(8,128)S(1)} %bitcast.36), channel_id=1, source_target_pairs={{0,1},{1,0},{2,3},{3,2},{4,5},{5,4},{6,7},{7,6},{8,9},{9,8},{10,11... | collective-permute-start | bytes 393224 | tf_op jit(solution)/shard_map/ppermute | solution.py:263
  4.7 1.0 %collective-permute-done = f32[2,2,2,2,16,128]{5,4,3,2,1,0:T(8,128)S(1)} collective-permute-done((f32[2,2,2,2,16,128]{5,4,3,2,1,0:T(8,128)S(1)}, f32[2,2,2,2,16,128]{5,4,3,2,1,0:T(8,128)S(1)}, u32[]{:S(2)}, u32[]{:S(2)}) %collective-permute-start) | collective-permute-done | bytes 131104 | tf_op jit(solution)/shard_map/ppermute | solution.py:263
  5.8 2.9 %collective-permute-start.1 = (f32[2,2,16,128]{3,2,1,0:T(8,128)S(1)}, f32[2,2,16,128]{3,2,1,0:T(8,128)S(1)}, u32[]{:S(2)}, u32[]{:S(2)}) collective-permute-start(f32[2,2,16,128]{3,2,1,0:T(8,128)S(1)} %get-tuple-element.13), channel_id=1, source_target_pairs={{0,2},{1,3},{2,0},{3,1},{4,6},{5,7},{6,4},{7,5},{8,10},{9,11},{10,... | collective-permute-start | bytes 98312 | tf_op jit(solution)/shard_map/ppermute | solution.py:263
  8.7 1.0 %collective-permute-start.3 = (f32[2,2,16,128]{3,2,1,0:T(8,128)S(1)}, f32[2,2,16,128]{3,2,1,0:T(8,128)S(1)}, u32[]{:S(2)}, u32[]{:S(2)}) collective-permute-start(f32[2,2,16,128]{3,2,1,0:T(8,128)S(1)} %get-tuple-element.14), channel_id=1, source_target_pairs={{0,11},{1,10},{2,9},{3,8},{4,15},{5,14},{6,13},{7,12},{8,3},{9,2},... | collective-permute-start | bytes 98312 | tf_op jit(solution)/shard_map/ppermute | solution.py:263
  9.7 0.2 %collective-permute-start.2 = (f32[2,2,16,128]{3,2,1,0:T(8,128)S(1)}, f32[2,2,16,128]{3,2,1,0:T(8,128)S(1)}, u32[]{:S(2)}, u32[]{:S(2)}) collective-permute-start(f32[2,2,16,128]{3,2,1,0:T(8,128)S(1)} %get-tuple-element.15), channel_id=1, source_target_pairs={{0,9},{1,8},{2,11},{3,10},{4,13},{5,12},{6,15},{7,14},{8,1},{9,0},... | collective-permute-start | bytes 98312 | tf_op jit(solution)/shard_map/ppermute | solution.py:263
  9.9 0.6 %collective-permute-done.1 = f32[2,2,16,128]{3,2,1,0:T(8,128)S(1)} collective-permute-done((f32[2,2,16,128]{3,2,1,0:T(8,128)S(1)}, f32[2,2,16,128]{3,2,1,0:T(8,128)S(1)}, u32[]{:S(2)}, u32[]{:S(2)}) %collective-permute-start.1) | collective-permute-done | bytes 32800 | tf_op jit(solution)/shard_map/ppermute | solution.py:263
  10.6 2.6 %collective-permute-done.3 = f32[2,2,16,128]{3,2,1,0:T(8,128)S(1)} collective-permute-done((f32[2,2,16,128]{3,2,1,0:T(8,128)S(1)}, f32[2,2,16,128]{3,2,1,0:T(8,128)S(1)}, u32[]{:S(2)}, u32[]{:S(2)}) %collective-permute-start.3) | collective-permute-done | bytes 32800 | tf_op jit(solution)/shard_map/ppermute | solution.py:263
  13.2 0.0 collective-permute-done.2
  13.2 1.6 %collective-permute-start.4 = (bf16[2,2,16,128]{3,2,0,1:T(8,128)(2,1)S(1)}, bf16[2,2,16,128]{3,2,0,1:T(8,128)(2,1)S(1)}, u32[]{:S(2)}, u32[]{:S(2)}) collective-permute-start(bf16[2,2,16,128]{3,2,0,1:T(8,128)(2,1)S(1)} %get-tuple-element.19), channel_id=1, source_target_pairs={{0,5},{1,4},{2,7},{3,6},{4,1},{5,0},{6,3},{7,2},{8,13},{9,12},{10,... | collective-permute-start | bytes 49160 | tf_op jit(solution)/shard_map/ppermute | solution.py:263
  14.9 1.6 %collective-permute-done.4 = bf16[2,2,16,128]{3,2,0,1:T(8,128)(2,1)S(1)} collective-permute-done((bf16[2,2,16,128]{3,2,0,1:T(8,128)(2,1)S(1)}, bf16[2,2,16,128]{3,2,0,1:T(8,128)(2,1)S(1)}, u32[]{:S(2)}, u32[]{:S(2)}) %collective-permute-start.4) | collective-permute-done | bytes 16416 | tf_op jit(solution)/shard_map/ppermute | solution.py:263
  16.5 2.7 %collective-permute-start.5 = (bf16[4,16,128]{2,1,0:T(8,128)(2,1)S(1)}, bf16[4,16,128]{2,1,0:T(8,128)(2,1)S(1)}, u32[]{:S(2)}, u32[]{:S(2)}) collective-permute-start(bf16[4,16,128]{2,1,0:T(8,128)(2,1)S(1)} %get-tuple-element.17), channel_id=1, source_target_pairs={{0,17},{1,16},{2,19},{3,18},{4,21},{5,20},{6,23},{7,22},{8,25},{9,... | collective-permute-start | bytes 49160 | tf_op jit(solution)/shard_map/ppermute | solution.py:263
  19.2 0.9 %spread.2.refs_1_ = bf16[64,16,128]{2,1,0:T(8,128)(2,1)} custom-call(f32[16,128]{1,0:T(8,128)S(1)} %get-tuple-element.8.j_in, f32[64,128]{1,0:T(8,128)S(1)} %get-tuple-element.9.i_in, bf16[4,16,128]{2,1,0:T(8,128)(2,1)S(1)} %get-tuple-element.16.refs_0_), custom_call_target="tpu_custom_call" | custom-call | flops 1000000 | bytes 131072 | tf_op jit(solution)/shard_map/spread/pallas_call | solution.py:210
  20.1 0.5 %collective-permute-done.5.refs_0_ = bf16[4,16,128]{2,1,0:T(8,128)(2,1)S(1)} collective-permute-done((bf16[4,16,128]{2,1,0:T(8,128)(2,1)S(1)}, bf16[4,16,128]{2,1,0:T(8,128)(2,1)S(1)}, u32[]{:S(2)}, u32[]{:S(2)}) %collective-permute-start.5) | collective-permute-done | bytes 16416 | tf_op jit(solution)/shard_map/ppermute | solution.py:263
  20.7 0.9 %spread.3 = bf16[64,16,128]{2,1,0:T(8,128)(2,1)} custom-call(f32[16,128]{1,0:T(8,128)S(1)} %get-tuple-element.8.j_in, f32[64,128]{1,0:T(8,128)S(1)} %get-tuple-element.9.i_in, bf16[4,16,128]{2,1,0:T(8,128)(2,1)S(1)} %collective-permute-done.5.refs_0_, bf16[64,16,128]{2,1,0:T(8,128)(2,1)} %spread.2.refs_1_), custom_call_target="tpu_custom_call", output_to_operand_aliasing={{}: (3, {})} | custom-call | flops 1000000 | bytes 131072 | tf_op jit(solution)/shard_map/spread/pallas_call | solution.py:210
  (8 shorter events, 0.1 us)
Async XLA Ops:
  4.2 1.5 %collective-permute-start = (f32[2,2,2,2,16,128]{5,4,3,2,1,0:T(8,128)S(1)}, f32[2,2,2,2,16,128]{5,4,3,2,1,0:T(8,128)S(1)}, u32[]{:S(2)}, u32[]{:S(2)}) collective-permute-start(f32[2,2,2,2,16,128]{5,4,3,2,1,0:T(8,128)S(1)} %bitcast.36), channel_id=1, source_target_pairs={{0,1},{1,0},{2,3},{3,2},{4,5},{5,4},{6,7},{7,6},{8,9},{9,8},{10,11... | collective-permute-start | bytes 393224 | tf_op jit(solution)/shard_map/ppermute | solution.py:263
  5.8 4.8 %collective-permute-start.1 = (f32[2,2,16,128]{3,2,1,0:T(8,128)S(1)}, f32[2,2,16,128]{3,2,1,0:T(8,128)S(1)}, u32[]{:S(2)}, u32[]{:S(2)}) collective-permute-start(f32[2,2,16,128]{3,2,1,0:T(8,128)S(1)} %get-tuple-element.13), channel_id=1, source_target_pairs={{0,2},{1,3},{2,0},{3,1},{4,6},{5,7},{6,4},{7,5},{8,10},{9,11},{10,... | collective-permute-start | bytes 98312 | tf_op jit(solution)/shard_map/ppermute | solution.py:263
  8.7 4.5 %collective-permute-start.3 = (f32[2,2,16,128]{3,2,1,0:T(8,128)S(1)}, f32[2,2,16,128]{3,2,1,0:T(8,128)S(1)}, u32[]{:S(2)}, u32[]{:S(2)}) collective-permute-start(f32[2,2,16,128]{3,2,1,0:T(8,128)S(1)} %get-tuple-element.14), channel_id=1, source_target_pairs={{0,11},{1,10},{2,9},{3,8},{4,15},{5,14},{6,13},{7,12},{8,3},{9,2},... | collective-permute-start | bytes 98312 | tf_op jit(solution)/shard_map/ppermute | solution.py:263
  9.7 3.5 %collective-permute-start.2 = (f32[2,2,16,128]{3,2,1,0:T(8,128)S(1)}, f32[2,2,16,128]{3,2,1,0:T(8,128)S(1)}, u32[]{:S(2)}, u32[]{:S(2)}) collective-permute-start(f32[2,2,16,128]{3,2,1,0:T(8,128)S(1)} %get-tuple-element.15), channel_id=1, source_target_pairs={{0,9},{1,8},{2,11},{3,10},{4,13},{5,12},{6,15},{7,14},{8,1},{9,0},... | collective-permute-start | bytes 98312 | tf_op jit(solution)/shard_map/ppermute | solution.py:263
  13.2 3.2 %collective-permute-start.4 = (bf16[2,2,16,128]{3,2,0,1:T(8,128)(2,1)S(1)}, bf16[2,2,16,128]{3,2,0,1:T(8,128)(2,1)S(1)}, u32[]{:S(2)}, u32[]{:S(2)}) collective-permute-start(bf16[2,2,16,128]{3,2,0,1:T(8,128)(2,1)S(1)} %get-tuple-element.19), channel_id=1, source_target_pairs={{0,5},{1,4},{2,7},{3,6},{4,1},{5,0},{6,3},{7,2},{8,13},{9,12},{10,... | collective-permute-start | bytes 49160 | tf_op jit(solution)/shard_map/ppermute | solution.py:263
  16.5 4.2 %collective-permute-start.5 = (bf16[4,16,128]{2,1,0:T(8,128)(2,1)S(1)}, bf16[4,16,128]{2,1,0:T(8,128)(2,1)S(1)}, u32[]{:S(2)}, u32[]{:S(2)}) collective-permute-start(bf16[4,16,128]{2,1,0:T(8,128)(2,1)S(1)} %get-tuple-element.17), channel_id=1, source_target_pairs={{0,17},{1,16},{2,19},{3,18},{4,21},{5,20},{6,23},{7,22},{8,25},{9,... | collective-permute-start | bytes 49160 | tf_op jit(solution)/shard_map/ppermute | solution.py:263

commit v4 on v3

--- a/solution.py
+++ b/solution.py
@@ -48,6 +48,7 @@
 OWNERS = 8
 REDS = 4
 V_CHUNKS = 2
+BY_PRODUCT = 2
 
 
 def place(offset):
@@ -108,7 +109,6 @@
         return value
 
     occ_j = [column(8 * g) for g in range(occupied // 8)]
-    occ_j16 = jnp.concatenate(occ_j, 0).astype(F32).astype(BF16)
     occ_i = [occ[pair * rows + i] for i in range(rows)]
 
     j_rows = occupied // REDS
@@ -123,39 +123,57 @@
         jnp.broadcast_to(vir[pl.ds(LANES * n, LANES)].reshape(1, LANES), (8, LANES))
         for n in range(pieces)
     ]
-    block_row = (lax.broadcasted_iota(I32, (LANES, LANES), 0) // BLOCK).astype(F32).astype(BF16)
+    sub_block = lax.broadcasted_iota(I32, (BLOCK, LANES), 0) // BLOCK
+    block_rows = [(sub_block + b).astype(F32).astype(BF16) for b in range(LABELS)]
     labels, masks = [], []
-    for q in range(depth // LANES):
-        index = cd[:, pl.ds(q * LANES, LANES)]
-        index = jnp.concatenate([index, jnp.zeros((6, LANES), I32)], 0)
+    for z in range(depth // LANES // 4):
+        index = jnp.concatenate([cd[:, pl.ds((4 * z + u) * LANES, LANES)] for u in range(4)], 0)
         within, piece = index % LANES, index // LANES
         found = jnp.take_along_axis(table[0], within, axis=1)
         for n in range(1, pieces):
             found = jnp.where(piece == n, jnp.take_along_axis(table[n], within, axis=1), found)
-        label = found[0:1] ^ found[1:2]
-        labels.append(label)
-        spread = jnp.broadcast_to(label, (LANES, LANES)).astype(F32).astype(BF16)
-        masks.append(jnp.where(spread == block_row, one, zero).T)
-
+        found = (found ^ pltpu.roll(found, 7, 0)).astype(F32)
+        for u in range(4):
+            label = jnp.broadcast_to(found[2 * u : 2 * u + 1], (BLOCK, LANES)).astype(BF16)
+            labels.append(label)
+            own = [jnp.where(label == row, one, zero) for row in block_rows]
+            masks.append(jnp.concatenate(own, 0).T)
+    own_labels = [
+        [
+            (jnp.concatenate(occ_j[g : g + 2], 0) ^ occ_i[i]).astype(F32).astype(BF16)
+            for g in range(0, occupied // 8, 2)
+        ]
+        for i in range(rows)
+    ]
+
+    turned = OWNERS - BY_PRODUCT
+    row = lax.broadcasted_iota(I32, (BY_PRODUCT * LANES, LANES), 0)
+    lane = lax.broadcasted_iota(I32, (BY_PRODUCT * LANES, LANES), 1)
+    target = (row + (row // LANES + turned) * BLOCK) % LANES
+    permutation = jnp.where(target == lane, 1.0, 0.0).astype(BF16)
     for c in range(V_CHUNKS):
         v_copies[c].wait()
         for q in range(c * span // LANES, (c + 1) * span // LANES):
             ks = pl.ds(q * LANES, LANES)
-            mask = masks[q] != zero
-            folded = jnp.where(mask, v_buf[ks, 0:LANES], zero)
-            for p in range(1, OWNERS):
-                part = jnp.where(mask, v_buf[ks, pl.ds(p * LANES, LANES)], zero)
-                folded = folded + turn(part, p)
-            w_buf[ks, :] = folded
+            parts = [masks[q] * v_buf[ks, pl.ds(p * LANES, LANES)] for p in range(OWNERS)]
+            folded = parts[0]
+            for p in range(1, turned):
+                folded = folded + turn(parts[p], p)
+            rest = jnp.concatenate(parts[turned:], 1)
+            rest = jnp.dot(rest, permutation, preferred_element_type=F32).astype(BF16)
+            w_buf[ks, :] = folded + rest
 
     t_copy.wait()
     masked = []
     for i in range(rows):
         row = []
         for q in range(depth // LANES):
-            wanted = jnp.broadcast_to(labels[q] ^ occ_i[i], (occupied, LANES))
-            wanted = wanted.astype(F32).astype(BF16)
-            row.append(jnp.where(wanted == occ_j16, t_buf[i, :, pl.ds(q * LANES, LANES)], zero))
+            group = t_buf[i, :, pl.ds(q * LANES, LANES)]
+            kept = [
+                jnp.where(labels[q] == own, group[g * BLOCK : (g + 1) * BLOCK], zero)
+                for g, own in enumerate(own_labels[i])
+            ]
+            row.append(jnp.concatenate(kept, 0))
         masked.append(jnp.concatenate(row, 1))
     total[...] = jnp.dot(
         jnp.concatenate(masked, 0), w_buf[...], preferred_element_type=F32
@@ -184,16 +202,10 @@
     sources = [(ref, k, a) for ref, of in zip(arrays, offsets) for k, a in enumerate(of)]
     copies = []
     for n, (ref, k, a) in enumerate(sources):
-        level = [ref[k]]
-        for b in (2, 1, 0):
-            level = [
-                jnp.where(bits[b], *((v, turn(v, -(2**b))) if upper else (turn(v, 2**b), v)))
-                for v in level
-                for upper in (False, True)
-            ]
+        skewed = pick([turn(ref[k], d) for d in range(LABELS)], bits)
         for i in range(8):
             wanted = jnp.broadcast_to(i_in[pl.ds(8 * a + i, 1), :], j_side.shape).astype(BF16)
-            buf[n, i] = jnp.where(wanted == j_side, level[i], jnp.zeros((), BF16))
+            buf[n, i] = jnp.where(wanted == j_side, skewed[-i % LABELS], jnp.zeros((), BF16))
         copy = pltpu.make_async_copy(buf.at[n], out.at[pl.ds((pair ^ a) * 8, 8)], sem.at[n])
         copy.start()
         copies.append(copy)

time: 21.7 us -> 21.3 us (0.982)
  Pallas kernels: 6.01 us -> 5.47 us
    pallas_call x2, Pallas kernels: 1.83 us -> 1.53 us  [spread(): pl.pallas_call(functools.partial(spread_kernel, offsets), out_shape=jax.S...]
    pallas_call x1, Pallas kernels: 4.18 us -> 3.94 us  [fast(): pl.pallas_call(sums_kernel, out_shape=(jax.ShapeDtypeStruct((OWNERS * RED...]
where the time goes in v4:
time: 21.3 us; the launch traced here: 21.2 us
  starting transfers between devices  9.07 us (43%)
  waiting for transfers between devices  6.5 us (31%)
  Pallas kernels  5.47 us (26%)
    ppermute x6, starting transfers between devices, swap(): return lax.ppermute(block, ('pair', 'red'), pairs)  9.07 us
    ppermute x6, waiting for transfers between devices, swap(): return lax.ppermute(block, ('pair', 'red'), pairs)  6.5 us
    pallas_call x1, Pallas kernels, fast(): pl.pallas_call(sums_kernel, out_shape=(jax.ShapeDtypeStruct((OWNERS * RED...  3.94 us
    pallas_call x2, Pallas kernels, spread(): pl.pallas_call(functools.partial(spread_kernel, offsets), out_shape=jax.S...  1.53 us
  transfers between devices with their start and end apart: 6, of which 5 were waited for; matrix products, arithmetic and copies ran while one was open for 0% of the time, Pallas kernels for 4%

profile of v4, /device:TPU:0, one launch (start us, length us, event | category | flops | bytes accessed | tf_op | source)
XLA Modules:
  0.0 21.2 jit_solution(718457403256026022)
XLA Ops:
  0.0 3.9 %sums.1 = (f32[32,16,128]{2,1,0:T(8,128)S(1)}, f32[16,128]{1,0:T(8,128)S(1)}, f32[64,128]{1,0:T(8,128)S(1)}) custom-call(s32[64]{0:T(128)} %occ_hbm.1, s32[512]{0:T(512)} %vir_hbm.1, s32[2,2048]{1,0:T(2,128)} %cd_hbm.1, bf16[8,64,2048]{2,1,0:T(8,128)(2,1)} %t_hbm.1, bf16[2048,1024]{1,0:T(8,128)(2,1)} %v_hbm.1), custom_call_target="tpu_custom_call" | custom-call | tf_op jit(solution)/shard_map/sums/pallas_call | solution.py:248
  4.0 0.5 %collective-permute-start = (f32[2,2,2,2,16,128]{5,4,3,2,1,0:T(8,128)S(1)}, f32[2,2,2,2,16,128]{5,4,3,2,1,0:T(8,128)S(1)}, u32[]{:S(2)}, u32[]{:S(2)}) collective-permute-start(f32[2,2,2,2,16,128]{5,4,3,2,1,0:T(8,128)S(1)} %bitcast.36), channel_id=1, source_target_pairs={{0,1},{1,0},{2,3},{3,2},{4,5},{5,4},{6,7},{7,6},{8,9},{9,8},{10,11... | collective-permute-start | bytes 393224 | tf_op jit(solution)/shard_map/ppermute | solution.py:275
  4.5 1.0 %collective-permute-done = f32[2,2,2,2,16,128]{5,4,3,2,1,0:T(8,128)S(1)} collective-permute-done((f32[2,2,2,2,16,128]{5,4,3,2,1,0:T(8,128)S(1)}, f32[2,2,2,2,16,128]{5,4,3,2,1,0:T(8,128)S(1)}, u32[]{:S(2)}, u32[]{:S(2)}) %collective-permute-start) | collective-permute-done | bytes 131104 | tf_op jit(solution)/shard_map/ppermute | solution.py:275
  5.5 2.9 %collective-permute-start.1 = (f32[2,2,16,128]{3,2,1,0:T(8,128)S(1)}, f32[2,2,16,128]{3,2,1,0:T(8,128)S(1)}, u32[]{:S(2)}, u32[]{:S(2)}) collective-permute-start(f32[2,2,16,128]{3,2,1,0:T(8,128)S(1)} %get-tuple-element.13), channel_id=1, source_target_pairs={{0,2},{1,3},{2,0},{3,1},{4,6},{5,7},{6,4},{7,5},{8,10},{9,11},{10,... | collective-permute-start | bytes 98312 | tf_op jit(solution)/shard_map/ppermute | solution.py:275
  8.4 1.0 %collective-permute-start.3 = (f32[2,2,16,128]{3,2,1,0:T(8,128)S(1)}, f32[2,2,16,128]{3,2,1,0:T(8,128)S(1)}, u32[]{:S(2)}, u32[]{:S(2)}) collective-permute-start(f32[2,2,16,128]{3,2,1,0:T(8,128)S(1)} %get-tuple-element.14), channel_id=1, source_target_pairs={{0,11},{1,10},{2,9},{3,8},{4,15},{5,14},{6,13},{7,12},{8,3},{9,2},... | collective-permute-start | bytes 98312 | tf_op jit(solution)/shard_map/ppermute | solution.py:275
  9.5 0.2 %collective-permute-start.2 = (f32[2,2,16,128]{3,2,1,0:T(8,128)S(1)}, f32[2,2,16,128]{3,2,1,0:T(8,128)S(1)}, u32[]{:S(2)}, u32[]{:S(2)}) collective-permute-start(f32[2,2,16,128]{3,2,1,0:T(8,128)S(1)} %get-tuple-element.15), channel_id=1, source_target_pairs={{0,9},{1,8},{2,11},{3,10},{4,13},{5,12},{6,15},{7,14},{8,1},{9,0},... | collective-permute-start | bytes 98312 | tf_op jit(solution)/shard_map/ppermute | solution.py:275
  9.7 0.6 %collective-permute-done.1 = f32[2,2,16,128]{3,2,1,0:T(8,128)S(1)} collective-permute-done((f32[2,2,16,128]{3,2,1,0:T(8,128)S(1)}, f32[2,2,16,128]{3,2,1,0:T(8,128)S(1)}, u32[]{:S(2)}, u32[]{:S(2)}) %collective-permute-start.1) | collective-permute-done | bytes 32800 | tf_op jit(solution)/shard_map/ppermute | solution.py:275
  10.3 2.6 %collective-permute-done.3 = f32[2,2,16,128]{3,2,1,0:T(8,128)S(1)} collective-permute-done((f32[2,2,16,128]{3,2,1,0:T(8,128)S(1)}, f32[2,2,16,128]{3,2,1,0:T(8,128)S(1)}, u32[]{:S(2)}, u32[]{:S(2)}) %collective-permute-start.3) | collective-permute-done | bytes 32800 | tf_op jit(solution)/shard_map/ppermute | solution.py:275
  13.0 0.0 collective-permute-done.2
  13.0 1.7 %collective-permute-start.4 = (bf16[2,2,16,128]{3,2,0,1:T(8,128)(2,1)S(1)}, bf16[2,2,16,128]{3,2,0,1:T(8,128)(2,1)S(1)}, u32[]{:S(2)}, u32[]{:S(2)}) collective-permute-start(bf16[2,2,16,128]{3,2,0,1:T(8,128)(2,1)S(1)} %get-tuple-element.19), channel_id=1, source_target_pairs={{0,5},{1,4},{2,7},{3,6},{4,1},{5,0},{6,3},{7,2},{8,13},{9,12},{10,... | collective-permute-start | bytes 49160 | tf_op jit(solution)/shard_map/ppermute | solution.py:275
  14.7 1.6 %collective-permute-done.4 = bf16[2,2,16,128]{3,2,0,1:T(8,128)(2,1)S(1)} collective-permute-done((bf16[2,2,16,128]{3,2,0,1:T(8,128)(2,1)S(1)}, bf16[2,2,16,128]{3,2,0,1:T(8,128)(2,1)S(1)}, u32[]{:S(2)}, u32[]{:S(2)}) %collective-permute-start.4) | collective-permute-done | bytes 16416 | tf_op jit(solution)/shard_map/ppermute | solution.py:275
  16.2 2.7 %collective-permute-start.5 = (bf16[4,16,128]{2,1,0:T(8,128)(2,1)S(1)}, bf16[4,16,128]{2,1,0:T(8,128)(2,1)S(1)}, u32[]{:S(2)}, u32[]{:S(2)}) collective-permute-start(bf16[4,16,128]{2,1,0:T(8,128)(2,1)S(1)} %get-tuple-element.17), channel_id=1, source_target_pairs={{0,17},{1,16},{2,19},{3,18},{4,21},{5,20},{6,23},{7,22},{8,25},{9,... | collective-permute-start | bytes 49160 | tf_op jit(solution)/shard_map/ppermute | solution.py:275
  19.0 0.8 %spread.2.refs_1_ = bf16[64,16,128]{2,1,0:T(8,128)(2,1)} custom-call(f32[16,128]{1,0:T(8,128)S(1)} %get-tuple-element.8.j_in, f32[64,128]{1,0:T(8,128)S(1)} %get-tuple-element.9.i_in, bf16[4,16,128]{2,1,0:T(8,128)(2,1)S(1)} %get-tuple-element.16.refs_0_), custom_call_target="tpu_custom_call" | custom-call | flops 1000000 | bytes 131072 | tf_op jit(solution)/shard_map/spread/pallas_call | solution.py:222
  19.7 0.7 %collective-permute-done.5.refs_0_ = bf16[4,16,128]{2,1,0:T(8,128)(2,1)S(1)} collective-permute-done((bf16[4,16,128]{2,1,0:T(8,128)(2,1)S(1)}, bf16[4,16,128]{2,1,0:T(8,128)(2,1)S(1)}, u32[]{:S(2)}, u32[]{:S(2)}) %collective-permute-start.5) | collective-permute-done | bytes 16416 | tf_op jit(solution)/shard_map/ppermute | solution.py:275
  20.4 0.8 %spread.3 = bf16[64,16,128]{2,1,0:T(8,128)(2,1)} custom-call(f32[16,128]{1,0:T(8,128)S(1)} %get-tuple-element.8.j_in, f32[64,128]{1,0:T(8,128)S(1)} %get-tuple-element.9.i_in, bf16[4,16,128]{2,1,0:T(8,128)(2,1)S(1)} %collective-permute-done.5.refs_0_, bf16[64,16,128]{2,1,0:T(8,128)(2,1)} %spread.2.refs_1_), custom_call_target="tpu_custom_call", output_to_operand_aliasing={{}: (3, {})} | custom-call | flops 1000000 | bytes 131072 | tf_op jit(solution)/shard_map/spread/pallas_call | solution.py:222
  (8 shorter events, 0.1 us)
Async XLA Ops:
  4.0 1.5 %collective-permute-start = (f32[2,2,2,2,16,128]{5,4,3,2,1,0:T(8,128)S(1)}, f32[2,2,2,2,16,128]{5,4,3,2,1,0:T(8,128)S(1)}, u32[]{:S(2)}, u32[]{:S(2)}) collective-permute-start(f32[2,2,2,2,16,128]{5,4,3,2,1,0:T(8,128)S(1)} %bitcast.36), channel_id=1, source_target_pairs={{0,1},{1,0},{2,3},{3,2},{4,5},{5,4},{6,7},{7,6},{8,9},{9,8},{10,11... | collective-permute-start | bytes 393224 | tf_op jit(solution)/shard_map/ppermute | solution.py:275
  5.5 4.8 %collective-permute-start.1 = (f32[2,2,16,128]{3,2,1,0:T(8,128)S(1)}, f32[2,2,16,128]{3,2,1,0:T(8,128)S(1)}, u32[]{:S(2)}, u32[]{:S(2)}) collective-permute-start(f32[2,2,16,128]{3,2,1,0:T(8,128)S(1)} %get-tuple-element.13), channel_id=1, source_target_pairs={{0,2},{1,3},{2,0},{3,1},{4,6},{5,7},{6,4},{7,5},{8,10},{9,11},{10,... | collective-permute-start | bytes 98312 | tf_op jit(solution)/shard_map/ppermute | solution.py:275
  8.4 4.5 %collective-permute-start.3 = (f32[2,2,16,128]{3,2,1,0:T(8,128)S(1)}, f32[2,2,16,128]{3,2,1,0:T(8,128)S(1)}, u32[]{:S(2)}, u32[]{:S(2)}) collective-permute-start(f32[2,2,16,128]{3,2,1,0:T(8,128)S(1)} %get-tuple-element.14), channel_id=1, source_target_pairs={{0,11},{1,10},{2,9},{3,8},{4,15},{5,14},{6,13},{7,12},{8,3},{9,2},... | collective-permute-start | bytes 98312 | tf_op jit(solution)/shard_map/ppermute | solution.py:275
  9.5 3.5 %collective-permute-start.2 = (f32[2,2,16,128]{3,2,1,0:T(8,128)S(1)}, f32[2,2,16,128]{3,2,1,0:T(8,128)S(1)}, u32[]{:S(2)}, u32[]{:S(2)}) collective-permute-start(f32[2,2,16,128]{3,2,1,0:T(8,128)S(1)} %get-tuple-element.15), channel_id=1, source_target_pairs={{0,9},{1,8},{2,11},{3,10},{4,13},{5,12},{6,15},{7,14},{8,1},{9,0},... | collective-permute-start | bytes 98312 | tf_op jit(solution)/shard_map/ppermute | solution.py:275
  13.0 3.2 %collective-permute-start.4 = (bf16[2,2,16,128]{3,2,0,1:T(8,128)(2,1)S(1)}, bf16[2,2,16,128]{3,2,0,1:T(8,128)(2,1)S(1)}, u32[]{:S(2)}, u32[]{:S(2)}) collective-permute-start(bf16[2,2,16,128]{3,2,0,1:T(8,128)(2,1)S(1)} %get-tuple-element.19), channel_id=1, source_target_pairs={{0,5},{1,4},{2,7},{3,6},{4,1},{5,0},{6,3},{7,2},{8,13},{9,12},{10,... | collective-permute-start | bytes 49160 | tf_op jit(solution)/shard_map/ppermute | solution.py:275
  16.2 4.2 %collective-permute-start.5 = (bf16[4,16,128]{2,1,0:T(8,128)(2,1)S(1)}, bf16[4,16,128]{2,1,0:T(8,128)(2,1)S(1)}, u32[]{:S(2)}, u32[]{:S(2)}) collective-permute-start(bf16[4,16,128]{2,1,0:T(8,128)(2,1)S(1)} %get-tuple-element.17), channel_id=1, source_target_pairs={{0,17},{1,16},{2,19},{3,18},{4,21},{5,20},{6,23},{7,22},{8,25},{9,... | collective-permute-start | bytes 49160 | tf_op jit(solution)/shard_map/ppermute | solution.py:275

commit v5 on v4

--- a/solution.py
+++ b/solution.py
@@ -194,47 +194,52 @@
             sums[to, pl.ds(g * 8 % j_rows, 8), :] = held[p]
 
 
-def spread_kernel(offsets, j_in, i_in, *refs):
-    arrays, (out, buf, sem) = refs[: len(offsets)], refs[-3:]
+def turned_blocks(block, bits):
+    skewed = pick([turn(block, d) for d in range(LABELS)], bits)
+    return [skewed[-i % LABELS] for i in range(LABELS)]
+
+
+def send_rows(blocks, offsets, masks, out, buf, sem):
     pair = lax.axis_index("pair")
+    bits = bits_of(lax.broadcasted_iota(I32, blocks.shape[1:], 1) // BLOCK)
+    for n, a in enumerate(offsets):
+        for i, block in enumerate(turned_blocks(blocks[n], bits)):
+            buf[n, i] = block * masks(n, i)
+        rows = out.at[pl.ds((pair ^ a) * 8, 8)]
+        pltpu.make_async_copy(buf.at[n], rows, sem).start()
+    return pltpu.make_async_copy(buf, buf, sem)
+
+
+def first_kernel(offsets, later, blocks, j_in, i_in, out, later_masks, buf, sem):
     j_side = j_in[...].astype(BF16)
-    bits = bits_of(lax.broadcasted_iota(I32, j_side.shape, 1) // BLOCK)
-    sources = [(ref, k, a) for ref, of in zip(arrays, offsets) for k, a in enumerate(of)]
-    copies = []
-    for n, (ref, k, a) in enumerate(sources):
-        skewed = pick([turn(ref[k], d) for d in range(LABELS)], bits)
+
+    def mask(a, i):
+        wanted = jnp.broadcast_to(i_in[pl.ds(8 * a + i, 1), :], j_side.shape).astype(BF16)
+        return jnp.where(wanted == j_side, jnp.ones((), BF16), jnp.zeros((), BF16))
+
+    all_rows = send_rows(blocks, offsets, lambda n, i: mask(offsets[n], i), out, buf, sem)
+    for n, a in enumerate(later):
         for i in range(8):
-            wanted = jnp.broadcast_to(i_in[pl.ds(8 * a + i, 1), :], j_side.shape).astype(BF16)
-            buf[n, i] = jnp.where(wanted == j_side, skewed[-i % LABELS], jnp.zeros((), BF16))
-        copy = pltpu.make_async_copy(buf.at[n], out.at[pl.ds((pair ^ a) * 8, 8)], sem.at[n])
-        copy.start()
-        copies.append(copy)
-    for copy in copies:
-        copy.wait()
-
-
-def spread(j_side, i_side, blocks, so_far=None):
-    offsets, arrays = [of for of, _ in blocks], [array for _, array in blocks]
-    count = sum(len(of) for of in offsets)
-    occupied, j_rows = i_side.shape[0], j_side.shape[0]
-    vmem, hbm = pl.BlockSpec(memory_space=pltpu.VMEM), pl.BlockSpec(memory_space=pltpu.HBM)
-    earlier = [] if so_far is None else [so_far]
+            later_masks[n, i] = mask(a, i)
+    all_rows.wait()
+
+
+def last_kernel(offsets, blocks, masks, so_far, out, buf, sem):
+    send_rows(blocks, offsets, lambda n, i: masks[n, i], out, buf, sem).wait()
+
+
+def spread(kernel, operands, in_specs, out_shape, out_specs, shape, **more):
     return pl.pallas_call(
-        functools.partial(spread_kernel, offsets),
-        out_shape=jax.ShapeDtypeStruct((occupied, j_rows, LANES), BF16),
-        in_specs=[vmem] * (2 + len(arrays)) + [hbm] * len(earlier),
-        out_specs=hbm,
-        scratch_shapes=[
-            pltpu.VMEM((count, 8, j_rows, LANES), BF16),
-            pltpu.SemaphoreType.DMA((count,)),
-        ],
-        input_output_aliases={2 + len(arrays): 0} if earlier else {},
+        kernel,
+        out_shape=out_shape,
+        in_specs=in_specs,
+        out_specs=out_specs,
+        scratch_shapes=[pltpu.VMEM(shape, BF16), pltpu.SemaphoreType.DMA],
         compiler_params=pltpu.CompilerParams(vmem_limit_bytes=8 * 2**20),
-        cost_estimate=pl.CostEstimate(
-            flops=10**6, bytes_accessed=2 * count * 8 * j_rows * LANES, transcendentals=0
-        ),
+        cost_estimate=pl.CostEstimate(flops=10**6, bytes_accessed=2**18, transcendentals=0),
         name="spread",
-    )(j_side, i_side, *arrays, *earlier)
+        **more,
+    )(*operands)
 
 
 def in_hbm(*arrays):
@@ -283,8 +288,17 @@
     done = jnp.stack([(chip[0, 0] + across).astype(BF16), (low + corner).astype(BF16)])
     both = jnp.stack([done[:, 0], swap(done[:, 1], Y)]).reshape(4, 2, j_rows, LANES)
     high = swap(both[:, 1], HIGH)
-    out = spread(j_side, i_side, [((0, 2, 1, 3), both[:, 0])])
-    return spread(j_side, i_side, [((4, 6, 5, 7), high)], out)
+    shape = (4, 8, j_rows, LANES)
+    result = jax.ShapeDtypeStruct((occupied, j_rows, LANES), BF16)
+    near, far = (0, 2, 1, 3), (4, 6, 5, 7)
+    out, masks = spread(
+        functools.partial(first_kernel, near, far), (both[:, 0], j_side, i_side), [vmem] * 3,
+        (result, jax.ShapeDtypeStruct(shape, BF16)), (hbm, vmem), shape,
+    )
+    return spread(
+        functools.partial(last_kernel, far), (high, masks, out), [vmem, vmem, hbm],
+        result, hbm, shape, input_output_aliases={2: 0},
+    )
 
 
 def solution(mesh):

time: 21.3 us -> 21.3 us (level)
  transfers between devices with their start and end apart: 6 -> 6, of which waited for: 5 -> 5; matrix products, arithmetic and copies ran while one was open for 0% -> 0% of each run, Pallas kernels for 4% -> 3%
where the time goes in v5:
time: 21.3 us; the launch traced here: 21.1 us
  starting transfers between devices  9.07 us (43%)
  waiting for transfers between devices  6.53 us (31%)
  Pallas kernels  5.41 us (25%)
    ppermute x6, starting transfers between devices, swap(): return lax.ppermute(block, ('pair', 'red'), pairs)  9.07 us
    ppermute x6, waiting for transfers between devices, swap(): return lax.ppermute(block, ('pair', 'red'), pairs)  6.53 us
    pallas_call x1, Pallas kernels, fast(): pl.pallas_call(sums_kernel, out_shape=(jax.ShapeDtypeStruct((OWNERS * RED...  3.94 us
    pallas_call x2, Pallas kernels, spread(): pl.pallas_call(kernel, out_shape=out_shape, in_specs=in_specs, out_specs=...  1.48 us
  transfers between devices with their start and end apart: 6, of which 5 were waited for; matrix products, arithmetic and copies ran while one was open for 0% of the time, Pallas kernels for 3%

profile of v5, /device:TPU:0, one launch (start us, length us, event | category | flops | bytes accessed | tf_op | source)
XLA Modules:
  0.0 21.1 jit_solution(13161740649615416046)
XLA Ops:
  0.0 3.9 %sums.1 = (f32[32,16,128]{2,1,0:T(8,128)S(1)}, f32[16,128]{1,0:T(8,128)S(1)}, f32[64,128]{1,0:T(8,128)S(1)}) custom-call(s32[64]{0:T(128)} %occ_hbm.1, s32[512]{0:T(512)} %vir_hbm.1, s32[2,2048]{1,0:T(2,128)} %cd_hbm.1, bf16[8,64,2048]{2,1,0:T(8,128)(2,1)} %t_hbm.1, bf16[2048,1024]{1,0:T(8,128)(2,1)} %v_hbm.1), custom_call_target="tpu_custom_call" | custom-call | tf_op jit(solution)/shard_map/sums/pallas_call | solution.py:253
  4.0 0.5 %collective-permute-start = (f32[2,2,2,2,16,128]{5,4,3,2,1,0:T(8,128)S(1)}, f32[2,2,2,2,16,128]{5,4,3,2,1,0:T(8,128)S(1)}, u32[]{:S(2)}, u32[]{:S(2)}) collective-permute-start(f32[2,2,2,2,16,128]{5,4,3,2,1,0:T(8,128)S(1)} %bitcast.36), channel_id=1, source_target_pairs={{0,1},{1,0},{2,3},{3,2},{4,5},{5,4},{6,7},{7,6},{8,9},{9,8},{10,11... | collective-permute-start | bytes 393224 | tf_op jit(solution)/shard_map/ppermute | solution.py:280
  4.5 1.0 %collective-permute-done = f32[2,2,2,2,16,128]{5,4,3,2,1,0:T(8,128)S(1)} collective-permute-done((f32[2,2,2,2,16,128]{5,4,3,2,1,0:T(8,128)S(1)}, f32[2,2,2,2,16,128]{5,4,3,2,1,0:T(8,128)S(1)}, u32[]{:S(2)}, u32[]{:S(2)}) %collective-permute-start) | collective-permute-done | bytes 131104 | tf_op jit(solution)/shard_map/ppermute | solution.py:280
  5.5 2.9 %collective-permute-start.1 = (f32[2,2,16,128]{3,2,1,0:T(8,128)S(1)}, f32[2,2,16,128]{3,2,1,0:T(8,128)S(1)}, u32[]{:S(2)}, u32[]{:S(2)}) collective-permute-start(f32[2,2,16,128]{3,2,1,0:T(8,128)S(1)} %get-tuple-element.17), channel_id=1, source_target_pairs={{0,2},{1,3},{2,0},{3,1},{4,6},{5,7},{6,4},{7,5},{8,10},{9,11},{10,... | collective-permute-start | bytes 98312 | tf_op jit(solution)/shard_map/ppermute | solution.py:280
  8.4 1.0 %collective-permute-start.3 = (f32[2,2,16,128]{3,2,1,0:T(8,128)S(1)}, f32[2,2,16,128]{3,2,1,0:T(8,128)S(1)}, u32[]{:S(2)}, u32[]{:S(2)}) collective-permute-start(f32[2,2,16,128]{3,2,1,0:T(8,128)S(1)} %get-tuple-element.18), channel_id=1, source_target_pairs={{0,11},{1,10},{2,9},{3,8},{4,15},{5,14},{6,13},{7,12},{8,3},{9,2},... | collective-permute-start | bytes 98312 | tf_op jit(solution)/shard_map/ppermute | solution.py:280
  9.5 0.2 %collective-permute-start.2 = (f32[2,2,16,128]{3,2,1,0:T(8,128)S(1)}, f32[2,2,16,128]{3,2,1,0:T(8,128)S(1)}, u32[]{:S(2)}, u32[]{:S(2)}) collective-permute-start(f32[2,2,16,128]{3,2,1,0:T(8,128)S(1)} %get-tuple-element.19), channel_id=1, source_target_pairs={{0,9},{1,8},{2,11},{3,10},{4,13},{5,12},{6,15},{7,14},{8,1},{9,0},... | collective-permute-start | bytes 98312 | tf_op jit(solution)/shard_map/ppermute | solution.py:280
  9.7 0.6 %collective-permute-done.1 = f32[2,2,16,128]{3,2,1,0:T(8,128)S(1)} collective-permute-done((f32[2,2,16,128]{3,2,1,0:T(8,128)S(1)}, f32[2,2,16,128]{3,2,1,0:T(8,128)S(1)}, u32[]{:S(2)}, u32[]{:S(2)}) %collective-permute-start.1) | collective-permute-done | bytes 32800 | tf_op jit(solution)/shard_map/ppermute | solution.py:280
  10.3 2.6 %collective-permute-done.3 = f32[2,2,16,128]{3,2,1,0:T(8,128)S(1)} collective-permute-done((f32[2,2,16,128]{3,2,1,0:T(8,128)S(1)}, f32[2,2,16,128]{3,2,1,0:T(8,128)S(1)}, u32[]{:S(2)}, u32[]{:S(2)}) %collective-permute-start.3) | collective-permute-done | bytes 32800 | tf_op jit(solution)/shard_map/ppermute | solution.py:280
  13.0 0.0 collective-permute-done.2
  13.0 1.7 %collective-permute-start.4 = (bf16[2,2,16,128]{3,2,0,1:T(8,128)(2,1)S(1)}, bf16[2,2,16,128]{3,2,0,1:T(8,128)(2,1)S(1)}, u32[]{:S(2)}, u32[]{:S(2)}) collective-permute-start(bf16[2,2,16,128]{3,2,0,1:T(8,128)(2,1)S(1)} %get-tuple-element.23), channel_id=1, source_target_pairs={{0,5},{1,4},{2,7},{3,6},{4,1},{5,0},{6,3},{7,2},{8,13},{9,12},{10,... | collective-permute-start | bytes 49160 | tf_op jit(solution)/shard_map/ppermute | solution.py:280
  14.7 1.6 %collective-permute-done.4 = bf16[2,2,16,128]{3,2,0,1:T(8,128)(2,1)S(1)} collective-permute-done((bf16[2,2,16,128]{3,2,0,1:T(8,128)(2,1)S(1)}, bf16[2,2,16,128]{3,2,0,1:T(8,128)(2,1)S(1)}, u32[]{:S(2)}, u32[]{:S(2)}) %collective-permute-start.4) | collective-permute-done | bytes 16416 | tf_op jit(solution)/shard_map/ppermute | solution.py:280
  16.2 2.7 %collective-permute-start.5 = (bf16[4,16,128]{2,1,0:T(8,128)(2,1)S(1)}, bf16[4,16,128]{2,1,0:T(8,128)(2,1)S(1)}, u32[]{:S(2)}, u32[]{:S(2)}) collective-permute-start(bf16[4,16,128]{2,1,0:T(8,128)(2,1)S(1)} %get-tuple-element.21), channel_id=1, source_target_pairs={{0,17},{1,16},{2,19},{3,18},{4,21},{5,20},{6,23},{7,22},{8,25},{9,... | collective-permute-start | bytes 49160 | tf_op jit(solution)/shard_map/ppermute | solution.py:280
  19.0 0.7 %spread.2 = (bf16[64,16,128]{2,1,0:T(8,128)(2,1)}, bf16[4,8,16,128]{3,2,1,0:T(8,128)(2,1)S(1)}) custom-call(bf16[4,16,128]{2,1,0:T(8,128)(2,1)S(1)} %get-tuple-element.20.blocks, f32[16,128]{1,0:T(8,128)S(1)} %get-tuple-element.11.j_in, f32[64,128]{1,0:T(8,128)S(1)} %get-tuple-element.12.i_in), custom_call_target="tpu_custom_call" | custom-call | flops 1000000 | bytes 262144 | tf_op jit(solution)/shard_map/spread/pallas_call | solution.py:232
  19.7 0.7 %collective-permute-done.5.blocks = bf16[4,16,128]{2,1,0:T(8,128)(2,1)S(1)} collective-permute-done((bf16[4,16,128]{2,1,0:T(8,128)(2,1)S(1)}, bf16[4,16,128]{2,1,0:T(8,128)(2,1)S(1)}, u32[]{:S(2)}, u32[]{:S(2)}) %collective-permute-start.5) | collective-permute-done | bytes 16416 | tf_op jit(solution)/shard_map/ppermute | solution.py:280
  20.4 0.7 %spread.3 = bf16[64,16,128]{2,1,0:T(8,128)(2,1)} custom-call(bf16[4,16,128]{2,1,0:T(8,128)(2,1)S(1)} %collective-permute-done.5.blocks, bf16[4,8,16,128]{3,2,1,0:T(8,128)(2,1)S(1)} %get-tuple-element.13.masks, bf16[64,16,128]{2,1,0:T(8,128)(2,1)} %get-tuple-element.14.so_far), custom_call_target="tpu_custom_call", output_to_operand_aliasing={{}: (2, {})} | custom-call | flops 1000000 | bytes 262144 | tf_op jit(solution)/shard_map/spread/pallas_call | solution.py:232
  (8 shorter events, 0.1 us)
Async XLA Ops:
  4.0 1.5 %collective-permute-start = (f32[2,2,2,2,16,128]{5,4,3,2,1,0:T(8,128)S(1)}, f32[2,2,2,2,16,128]{5,4,3,2,1,0:T(8,128)S(1)}, u32[]{:S(2)}, u32[]{:S(2)}) collective-permute-start(f32[2,2,2,2,16,128]{5,4,3,2,1,0:T(8,128)S(1)} %bitcast.36), channel_id=1, source_target_pairs={{0,1},{1,0},{2,3},{3,2},{4,5},{5,4},{6,7},{7,6},{8,9},{9,8},{10,11... | collective-permute-start | bytes 393224 | tf_op jit(solution)/shard_map/ppermute | solution.py:280
  5.5 4.8 %collective-permute-start.1 = (f32[2,2,16,128]{3,2,1,0:T(8,128)S(1)}, f32[2,2,16,128]{3,2,1,0:T(8,128)S(1)}, u32[]{:S(2)}, u32[]{:S(2)}) collective-permute-start(f32[2,2,16,128]{3,2,1,0:T(8,128)S(1)} %get-tuple-element.17), channel_id=1, source_target_pairs={{0,2},{1,3},{2,0},{3,1},{4,6},{5,7},{6,4},{7,5},{8,10},{9,11},{10,... | collective-permute-start | bytes 98312 | tf_op jit(solution)/shard_map/ppermute | solution.py:280
  8.4 4.5 %collective-permute-start.3 = (f32[2,2,16,128]{3,2,1,0:T(8,128)S(1)}, f32[2,2,16,128]{3,2,1,0:T(8,128)S(1)}, u32[]{:S(2)}, u32[]{:S(2)}) collective-permute-start(f32[2,2,16,128]{3,2,1,0:T(8,128)S(1)} %get-tuple-element.18), channel_id=1, source_target_pairs={{0,11},{1,10},{2,9},{3,8},{4,15},{5,14},{6,13},{7,12},{8,3},{9,2},... | collective-permute-start | bytes 98312 | tf_op jit(solution)/shard_map/ppermute | solution.py:280
  9.5 3.5 %collective-permute-start.2 = (f32[2,2,16,128]{3,2,1,0:T(8,128)S(1)}, f32[2,2,16,128]{3,2,1,0:T(8,128)S(1)}, u32[]{:S(2)}, u32[]{:S(2)}) collective-permute-start(f32[2,2,16,128]{3,2,1,0:T(8,128)S(1)} %get-tuple-element.19), channel_id=1, source_target_pairs={{0,9},{1,8},{2,11},{3,10},{4,13},{5,12},{6,15},{7,14},{8,1},{9,0},... | collective-permute-start | bytes 98312 | tf_op jit(solution)/shard_map/ppermute | solution.py:280
  13.0 3.2 %collective-permute-start.4 = (bf16[2,2,16,128]{3,2,0,1:T(8,128)(2,1)S(1)}, bf16[2,2,16,128]{3,2,0,1:T(8,128)(2,1)S(1)}, u32[]{:S(2)}, u32[]{:S(2)}) collective-permute-start(bf16[2,2,16,128]{3,2,0,1:T(8,128)(2,1)S(1)} %get-tuple-element.23), channel_id=1, source_target_pairs={{0,5},{1,4},{2,7},{3,6},{4,1},{5,0},{6,3},{7,2},{8,13},{9,12},{10,... | collective-permute-start | bytes 49160 | tf_op jit(solution)/shard_map/ppermute | solution.py:280
  16.2 4.2 %collective-permute-start.5 = (bf16[4,16,128]{2,1,0:T(8,128)(2,1)S(1)}, bf16[4,16,128]{2,1,0:T(8,128)(2,1)S(1)}, u32[]{:S(2)}, u32[]{:S(2)}) collective-permute-start(bf16[4,16,128]{2,1,0:T(8,128)(2,1)S(1)} %get-tuple-element.21), channel_id=1, source_target_pairs={{0,17},{1,16},{2,19},{3,18},{4,21},{5,20},{6,23},{7,22},{8,25},{9,... | collective-permute-start | bytes 49160 | tf_op jit(solution)/shard_map/ppermute | solution.py:280

commit v6 on v4

--- a/solution.py
+++ b/solution.py
@@ -200,17 +200,13 @@
     j_side = j_in[...].astype(BF16)
     bits = bits_of(lax.broadcasted_iota(I32, j_side.shape, 1) // BLOCK)
     sources = [(ref, k, a) for ref, of in zip(arrays, offsets) for k, a in enumerate(of)]
-    copies = []
     for n, (ref, k, a) in enumerate(sources):
         skewed = pick([turn(ref[k], d) for d in range(LABELS)], bits)
         for i in range(8):
             wanted = jnp.broadcast_to(i_in[pl.ds(8 * a + i, 1), :], j_side.shape).astype(BF16)
             buf[n, i] = jnp.where(wanted == j_side, skewed[-i % LABELS], jnp.zeros((), BF16))
-        copy = pltpu.make_async_copy(buf.at[n], out.at[pl.ds((pair ^ a) * 8, 8)], sem.at[n])
-        copy.start()
-        copies.append(copy)
-    for copy in copies:
-        copy.wait()
+        pltpu.make_async_copy(buf.at[n], out.at[pl.ds((pair ^ a) * 8, 8)], sem).start()
+    pltpu.make_async_copy(buf, buf, sem).wait()
 
 
 def spread(j_side, i_side, blocks, so_far=None):
@@ -226,7 +222,7 @@
         out_specs=hbm,
         scratch_shapes=[
             pltpu.VMEM((count, 8, j_rows, LANES), BF16),
-            pltpu.SemaphoreType.DMA((count,)),
+            pltpu.SemaphoreType.DMA,
         ],
         input_output_aliases={2 + len(arrays): 0} if earlier else {},
         compiler_params=pltpu.CompilerParams(vmem_limit_bytes=8 * 2**20),
@@ -281,10 +277,10 @@
     across = swap(chip[1, 0], X)
     corner = swap(chip[1, 1], X ^ LOW)
     done = jnp.stack([(chip[0, 0] + across).astype(BF16), (low + corner).astype(BF16)])
-    both = jnp.stack([done[:, 0], swap(done[:, 1], Y)]).reshape(4, 2, j_rows, LANES)
-    high = swap(both[:, 1], HIGH)
-    out = spread(j_side, i_side, [((0, 2, 1, 3), both[:, 0])])
-    return spread(j_side, i_side, [((4, 6, 5, 7), high)], out)
+    both = jnp.stack([done[:, :, 0], swap(done[:, :, 1], HIGH)]).reshape(4, 2, j_rows, LANES)
+    side = swap(both[:, 1], Y)
+    out = spread(j_side, i_side, [((0, 2, 4, 6), both[:, 0])])
+    return spread(j_side, i_side, [((1, 3, 5, 7), side)], out)
 
 
 def solution(mesh):

time: 21.3 us -> 21.3 us (level)
  transfers between devices with their start and end apart: 6 -> 6, of which waited for: 5 -> 5; matrix products, arithmetic and copies ran while one was open for 0% -> 0% of each run, Pallas kernels for 4% -> 3%
where the time goes in v6:
time: 21.3 us; the launch traced here: 21.2 us
  starting transfers between devices  9.04 us (42%)
  waiting for transfers between devices  6.55 us (31%)
  Pallas kernels  5.42 us (25%)
    ppermute x6, starting transfers between devices, swap(): return lax.ppermute(block, ('pair', 'red'), pairs)  9.04 us
    ppermute x6, waiting for transfers between devices, swap(): return lax.ppermute(block, ('pair', 'red'), pairs)  6.55 us
    pallas_call x1, Pallas kernels, fast(): pl.pallas_call(sums_kernel, out_shape=(jax.ShapeDtypeStruct((OWNERS * RED...  3.94 us
    pallas_call x2, Pallas kernels, spread(): pl.pallas_call(functools.partial(spread_kernel, offsets), out_shape=jax.S...  1.48 us
  transfers between devices with their start and end apart: 6, of which 5 were waited for; matrix products, arithmetic and copies ran while one was open for 0% of the time, Pallas kernels for 3%

profile of v6, /device:TPU:0, one launch (start us, length us, event | category | flops | bytes accessed | tf_op | source)
XLA Modules:
  0.0 21.2 jit_solution(15119014931458325885)
XLA Ops:
  0.0 3.9 %sums.1 = (f32[32,16,128]{2,1,0:T(8,128)S(1)}, f32[16,128]{1,0:T(8,128)S(1)}, f32[64,128]{1,0:T(8,128)S(1)}) custom-call(s32[64]{0:T(128)} %occ_hbm.1, s32[512]{0:T(512)} %vir_hbm.1, s32[2,2048]{1,0:T(2,128)} %cd_hbm.1, bf16[8,64,2048]{2,1,0:T(8,128)(2,1)} %t_hbm.1, bf16[2048,1024]{1,0:T(8,128)(2,1)} %v_hbm.1), custom_call_target="tpu_custom_call" | custom-call | tf_op jit(solution)/shard_map/sums/pallas_call | solution.py:244
  4.0 0.5 %collective-permute-start = (f32[2,2,2,2,16,128]{5,4,2,3,1,0:T(8,128)S(1)}, f32[2,2,2,2,16,128]{5,4,2,3,1,0:T(8,128)S(1)}, u32[]{:S(2)}, u32[]{:S(2)}) collective-permute-start(f32[2,2,2,2,16,128]{5,4,2,3,1,0:T(8,128)S(1)} %copy.7), channel_id=1, source_target_pairs={{0,1},{1,0},{2,3},{3,2},{4,5},{5,4},{6,7},{7,6},{8,9},{9,8},{10,11... | collective-permute-start | bytes 393224 | tf_op jit(solution)/shard_map/ppermute | solution.py:271
  4.5 1.0 %collective-permute-done = f32[2,2,2,2,16,128]{5,4,2,3,1,0:T(8,128)S(1)} collective-permute-done((f32[2,2,2,2,16,128]{5,4,2,3,1,0:T(8,128)S(1)}, f32[2,2,2,2,16,128]{5,4,2,3,1,0:T(8,128)S(1)}, u32[]{:S(2)}, u32[]{:S(2)}) %collective-permute-start) | collective-permute-done | bytes 131104 | tf_op jit(solution)/shard_map/ppermute | solution.py:271
  5.5 2.9 %collective-permute-start.1 = (f32[2,2,16,128]{3,2,0,1:T(8,128)S(1)}, f32[2,2,16,128]{3,2,0,1:T(8,128)S(1)}, u32[]{:S(2)}, u32[]{:S(2)}) collective-permute-start(f32[2,2,16,128]{3,2,0,1:T(8,128)S(1)} %get-tuple-element.13), channel_id=1, source_target_pairs={{0,2},{1,3},{2,0},{3,1},{4,6},{5,7},{6,4},{7,5},{8,10},{9,11},{10,... | collective-permute-start | bytes 98312 | tf_op jit(solution)/shard_map/ppermute | solution.py:271
  8.4 1.0 %collective-permute-start.3 = (f32[2,2,16,128]{3,2,0,1:T(8,128)S(1)}, f32[2,2,16,128]{3,2,0,1:T(8,128)S(1)}, u32[]{:S(2)}, u32[]{:S(2)}) collective-permute-start(f32[2,2,16,128]{3,2,0,1:T(8,128)S(1)} %get-tuple-element.14), channel_id=1, source_target_pairs={{0,11},{1,10},{2,9},{3,8},{4,15},{5,14},{6,13},{7,12},{8,3},{9,2},... | collective-permute-start | bytes 98312 | tf_op jit(solution)/shard_map/ppermute | solution.py:271
  9.5 0.2 %collective-permute-start.2 = (f32[2,2,16,128]{3,2,0,1:T(8,128)S(1)}, f32[2,2,16,128]{3,2,0,1:T(8,128)S(1)}, u32[]{:S(2)}, u32[]{:S(2)}) collective-permute-start(f32[2,2,16,128]{3,2,0,1:T(8,128)S(1)} %get-tuple-element.15), channel_id=1, source_target_pairs={{0,9},{1,8},{2,11},{3,10},{4,13},{5,12},{6,15},{7,14},{8,1},{9,0},... | collective-permute-start | bytes 98312 | tf_op jit(solution)/shard_map/ppermute | solution.py:271
  9.7 0.6 %collective-permute-done.1 = f32[2,2,16,128]{3,2,0,1:T(8,128)S(1)} collective-permute-done((f32[2,2,16,128]{3,2,0,1:T(8,128)S(1)}, f32[2,2,16,128]{3,2,0,1:T(8,128)S(1)}, u32[]{:S(2)}, u32[]{:S(2)}) %collective-permute-start.1) | collective-permute-done | bytes 32800 | tf_op jit(solution)/shard_map/ppermute | solution.py:271
  10.4 2.6 %collective-permute-done.3 = f32[2,2,16,128]{3,2,0,1:T(8,128)S(1)} collective-permute-done((f32[2,2,16,128]{3,2,0,1:T(8,128)S(1)}, f32[2,2,16,128]{3,2,0,1:T(8,128)S(1)}, u32[]{:S(2)}, u32[]{:S(2)}) %collective-permute-start.3) | collective-permute-done | bytes 32800 | tf_op jit(solution)/shard_map/ppermute | solution.py:271
  13.0 0.0 collective-permute-done.2
  13.0 2.7 %collective-permute-start.4 = (bf16[2,2,16,128]{3,2,0,1:T(8,128)(2,1)S(1)}, bf16[2,2,16,128]{3,2,0,1:T(8,128)(2,1)S(1)}, u32[]{:S(2)}, u32[]{:S(2)}) collective-permute-start(bf16[2,2,16,128]{3,2,0,1:T(8,128)(2,1)S(1)} %get-tuple-element.19), channel_id=1, source_target_pairs={{0,17},{1,16},{2,19},{3,18},{4,21},{5,20},{6,23},{7,22},{8,25},{9,... | collective-permute-start | bytes 49160 | tf_op jit(solution)/shard_map/ppermute | solution.py:271
  15.7 1.4 %collective-permute-done.4 = bf16[2,2,16,128]{3,2,0,1:T(8,128)(2,1)S(1)} collective-permute-done((bf16[2,2,16,128]{3,2,0,1:T(8,128)(2,1)S(1)}, bf16[2,2,16,128]{3,2,0,1:T(8,128)(2,1)S(1)}, u32[]{:S(2)}, u32[]{:S(2)}) %collective-permute-start.4) | collective-permute-done | bytes 16416 | tf_op jit(solution)/shard_map/ppermute | solution.py:271
  17.2 1.6 %collective-permute-start.5 = (bf16[4,16,128]{2,1,0:T(8,128)(2,1)S(1)}, bf16[4,16,128]{2,1,0:T(8,128)(2,1)S(1)}, u32[]{:S(2)}, u32[]{:S(2)}) collective-permute-start(bf16[4,16,128]{2,1,0:T(8,128)(2,1)S(1)} %get-tuple-element.17), channel_id=1, source_target_pairs={{0,5},{1,4},{2,7},{3,6},{4,1},{5,0},{6,3},{7,2},{8,13},{9,12},{10,... | collective-permute-start | bytes 49160 | tf_op jit(solution)/shard_map/ppermute | solution.py:271
  18.8 0.7 %spread.2.refs_1_ = bf16[64,16,128]{2,1,0:T(8,128)(2,1)} custom-call(f32[16,128]{1,0:T(8,128)S(1)} %get-tuple-element.8.j_in, f32[64,128]{1,0:T(8,128)S(1)} %get-tuple-element.9.i_in, bf16[4,16,128]{2,1,0:T(8,128)(2,1)S(1)} %get-tuple-element.16.refs_0_), custom_call_target="tpu_custom_call" | custom-call | flops 1000000 | bytes 131072 | tf_op jit(solution)/shard_map/spread/pallas_call | solution.py:218
  19.6 0.9 %collective-permute-done.5.refs_0_ = bf16[4,16,128]{2,1,0:T(8,128)(2,1)S(1)} collective-permute-done((bf16[4,16,128]{2,1,0:T(8,128)(2,1)S(1)}, bf16[4,16,128]{2,1,0:T(8,128)(2,1)S(1)}, u32[]{:S(2)}, u32[]{:S(2)}) %collective-permute-start.5) | collective-permute-done | bytes 16416 | tf_op jit(solution)/shard_map/ppermute | solution.py:271
  20.4 0.7 %spread.3 = bf16[64,16,128]{2,1,0:T(8,128)(2,1)} custom-call(f32[16,128]{1,0:T(8,128)S(1)} %get-tuple-element.8.j_in, f32[64,128]{1,0:T(8,128)S(1)} %get-tuple-element.9.i_in, bf16[4,16,128]{2,1,0:T(8,128)(2,1)S(1)} %collective-permute-done.5.refs_0_, bf16[64,16,128]{2,1,0:T(8,128)(2,1)} %spread.2.refs_1_), custom_call_target="tpu_custom_call", output_to_operand_aliasing={{}: (3, {})} | custom-call | flops 1000000 | bytes 131072 | tf_op jit(solution)/shard_map/spread/pallas_call | solution.py:218
  (9 shorter events, 0.1 us)
Async XLA Ops:
  4.0 1.5 %collective-permute-start = (f32[2,2,2,2,16,128]{5,4,2,3,1,0:T(8,128)S(1)}, f32[2,2,2,2,16,128]{5,4,2,3,1,0:T(8,128)S(1)}, u32[]{:S(2)}, u32[]{:S(2)}) collective-permute-start(f32[2,2,2,2,16,128]{5,4,2,3,1,0:T(8,128)S(1)} %copy.7), channel_id=1, source_target_pairs={{0,1},{1,0},{2,3},{3,2},{4,5},{5,4},{6,7},{7,6},{8,9},{9,8},{10,11... | collective-permute-start | bytes 393224 | tf_op jit(solution)/shard_map/ppermute | solution.py:271
  5.5 4.8 %collective-permute-start.1 = (f32[2,2,16,128]{3,2,0,1:T(8,128)S(1)}, f32[2,2,16,128]{3,2,0,1:T(8,128)S(1)}, u32[]{:S(2)}, u32[]{:S(2)}) collective-permute-start(f32[2,2,16,128]{3,2,0,1:T(8,128)S(1)} %get-tuple-element.13), channel_id=1, source_target_pairs={{0,2},{1,3},{2,0},{3,1},{4,6},{5,7},{6,4},{7,5},{8,10},{9,11},{10,... | collective-permute-start | bytes 98312 | tf_op jit(solution)/shard_map/ppermute | solution.py:271
  8.4 4.5 %collective-permute-start.3 = (f32[2,2,16,128]{3,2,0,1:T(8,128)S(1)}, f32[2,2,16,128]{3,2,0,1:T(8,128)S(1)}, u32[]{:S(2)}, u32[]{:S(2)}) collective-permute-start(f32[2,2,16,128]{3,2,0,1:T(8,128)S(1)} %get-tuple-element.14), channel_id=1, source_target_pairs={{0,11},{1,10},{2,9},{3,8},{4,15},{5,14},{6,13},{7,12},{8,3},{9,2},... | collective-permute-start | bytes 98312 | tf_op jit(solution)/shard_map/ppermute | solution.py:271
  9.5 3.5 %collective-permute-start.2 = (f32[2,2,16,128]{3,2,0,1:T(8,128)S(1)}, f32[2,2,16,128]{3,2,0,1:T(8,128)S(1)}, u32[]{:S(2)}, u32[]{:S(2)}) collective-permute-start(f32[2,2,16,128]{3,2,0,1:T(8,128)S(1)} %get-tuple-element.15), channel_id=1, source_target_pairs={{0,9},{1,8},{2,11},{3,10},{4,13},{5,12},{6,15},{7,14},{8,1},{9,0},... | collective-permute-start | bytes 98312 | tf_op jit(solution)/shard_map/ppermute | solution.py:271
  13.0 4.2 %collective-permute-start.4 = (bf16[2,2,16,128]{3,2,0,1:T(8,128)(2,1)S(1)}, bf16[2,2,16,128]{3,2,0,1:T(8,128)(2,1)S(1)}, u32[]{:S(2)}, u32[]{:S(2)}) collective-permute-start(bf16[2,2,16,128]{3,2,0,1:T(8,128)(2,1)S(1)} %get-tuple-element.19), channel_id=1, source_target_pairs={{0,17},{1,16},{2,19},{3,18},{4,21},{5,20},{6,23},{7,22},{8,25},{9,... | collective-permute-start | bytes 49160 | tf_op jit(solution)/shard_map/ppermute | solution.py:271
  17.2 3.2 %collective-permute-start.5 = (bf16[4,16,128]{2,1,0:T(8,128)(2,1)S(1)}, bf16[4,16,128]{2,1,0:T(8,128)(2,1)S(1)}, u32[]{:S(2)}, u32[]{:S(2)}) collective-permute-start(bf16[4,16,128]{2,1,0:T(8,128)(2,1)S(1)} %get-tuple-element.17), channel_id=1, source_target_pairs={{0,5},{1,4},{2,7},{3,6},{4,1},{5,0},{6,3},{7,2},{8,13},{9,12},{10,... | collective-permute-start | bytes 49160 | tf_op jit(solution)/shard_map/ppermute | solution.py:271

commit v7 on v6

--- a/solution.py
+++ b/solution.py
@@ -48,7 +48,7 @@
 OWNERS = 8
 REDS = 4
 V_CHUNKS = 2
-BY_PRODUCT = 2
+BY_PRODUCT = 1
 
 
 def place(offset):

time: 21.3 us -> 21.3 us (level)
  no operation moved by 1% of the time
where the time goes in v7:
time: 21.3 us; the launch traced here: 21.2 us
  starting transfers between devices  9.04 us (42%)
  waiting for transfers between devices  6.55 us (31%)
  Pallas kernels  5.42 us (25%)
    ppermute x6, starting transfers between devices, swap(): return lax.ppermute(block, ('pair', 'red'), pairs)  9.04 us
    ppermute x6, waiting for transfers between devices, swap(): return lax.ppermute(block, ('pair', 'red'), pairs)  6.55 us
    pallas_call x1, Pallas kernels, fast(): pl.pallas_call(sums_kernel, out_shape=(jax.ShapeDtypeStruct((OWNERS * RED...  3.94 us
    pallas_call x2, Pallas kernels, spread(): pl.pallas_call(functools.partial(spread_kernel, offsets), out_shape=jax.S...  1.48 us
  transfers between devices with their start and end apart: 6, of which 5 were waited for; matrix products, arithmetic and copies ran while one was open for 0% of the time, Pallas kernels for 3%

profile of v7, /device:TPU:0, one launch (start us, length us, event | category | flops | bytes accessed | tf_op | source)
XLA Modules:
  0.0 21.2 jit_solution(1629122583522108853)
XLA Ops:
  0.0 3.9 %sums.1 = (f32[32,16,128]{2,1,0:T(8,128)S(1)}, f32[16,128]{1,0:T(8,128)S(1)}, f32[64,128]{1,0:T(8,128)S(1)}) custom-call(s32[64]{0:T(128)} %occ_hbm.1, s32[512]{0:T(512)} %vir_hbm.1, s32[2,2048]{1,0:T(2,128)} %cd_hbm.1, bf16[8,64,2048]{2,1,0:T(8,128)(2,1)} %t_hbm.1, bf16[2048,1024]{1,0:T(8,128)(2,1)} %v_hbm.1), custom_call_target="tpu_custom_call" | custom-call | tf_op jit(solution)/shard_map/sums/pallas_call | solution.py:244
  4.0 0.5 %collective-permute-start = (f32[2,2,2,2,16,128]{5,4,2,3,1,0:T(8,128)S(1)}, f32[2,2,2,2,16,128]{5,4,2,3,1,0:T(8,128)S(1)}, u32[]{:S(2)}, u32[]{:S(2)}) collective-permute-start(f32[2,2,2,2,16,128]{5,4,2,3,1,0:T(8,128)S(1)} %copy.7), channel_id=1, source_target_pairs={{0,1},{1,0},{2,3},{3,2},{4,5},{5,4},{6,7},{7,6},{8,9},{9,8},{10,11... | collective-permute-start | bytes 393224 | tf_op jit(solution)/shard_map/ppermute | solution.py:271
  4.5 1.0 %collective-permute-done = f32[2,2,2,2,16,128]{5,4,2,3,1,0:T(8,128)S(1)} collective-permute-done((f32[2,2,2,2,16,128]{5,4,2,3,1,0:T(8,128)S(1)}, f32[2,2,2,2,16,128]{5,4,2,3,1,0:T(8,128)S(1)}, u32[]{:S(2)}, u32[]{:S(2)}) %collective-permute-start) | collective-permute-done | bytes 131104 | tf_op jit(solution)/shard_map/ppermute | solution.py:271
  5.5 2.9 %collective-permute-start.1 = (f32[2,2,16,128]{3,2,0,1:T(8,128)S(1)}, f32[2,2,16,128]{3,2,0,1:T(8,128)S(1)}, u32[]{:S(2)}, u32[]{:S(2)}) collective-permute-start(f32[2,2,16,128]{3,2,0,1:T(8,128)S(1)} %get-tuple-element.13), channel_id=1, source_target_pairs={{0,2},{1,3},{2,0},{3,1},{4,6},{5,7},{6,4},{7,5},{8,10},{9,11},{10,... | collective-permute-start | bytes 98312 | tf_op jit(solution)/shard_map/ppermute | solution.py:271
  8.5 1.0 %collective-permute-start.3 = (f32[2,2,16,128]{3,2,0,1:T(8,128)S(1)}, f32[2,2,16,128]{3,2,0,1:T(8,128)S(1)}, u32[]{:S(2)}, u32[]{:S(2)}) collective-permute-start(f32[2,2,16,128]{3,2,0,1:T(8,128)S(1)} %get-tuple-element.14), channel_id=1, source_target_pairs={{0,11},{1,10},{2,9},{3,8},{4,15},{5,14},{6,13},{7,12},{8,3},{9,2},... | collective-permute-start | bytes 98312 | tf_op jit(solution)/shard_map/ppermute | solution.py:271
  9.5 0.2 %collective-permute-start.2 = (f32[2,2,16,128]{3,2,0,1:T(8,128)S(1)}, f32[2,2,16,128]{3,2,0,1:T(8,128)S(1)}, u32[]{:S(2)}, u32[]{:S(2)}) collective-permute-start(f32[2,2,16,128]{3,2,0,1:T(8,128)S(1)} %get-tuple-element.15), channel_id=1, source_target_pairs={{0,9},{1,8},{2,11},{3,10},{4,13},{5,12},{6,15},{7,14},{8,1},{9,0},... | collective-permute-start | bytes 98312 | tf_op jit(solution)/shard_map/ppermute | solution.py:271
  9.7 0.6 %collective-permute-done.1 = f32[2,2,16,128]{3,2,0,1:T(8,128)S(1)} collective-permute-done((f32[2,2,16,128]{3,2,0,1:T(8,128)S(1)}, f32[2,2,16,128]{3,2,0,1:T(8,128)S(1)}, u32[]{:S(2)}, u32[]{:S(2)}) %collective-permute-start.1) | collective-permute-done | bytes 32800 | tf_op jit(solution)/shard_map/ppermute | solution.py:271
  10.4 2.6 %collective-permute-done.3 = f32[2,2,16,128]{3,2,0,1:T(8,128)S(1)} collective-permute-done((f32[2,2,16,128]{3,2,0,1:T(8,128)S(1)}, f32[2,2,16,128]{3,2,0,1:T(8,128)S(1)}, u32[]{:S(2)}, u32[]{:S(2)}) %collective-permute-start.3) | collective-permute-done | bytes 32800 | tf_op jit(solution)/shard_map/ppermute | solution.py:271
  13.0 0.0 collective-permute-done.2
  13.0 2.7 %collective-permute-start.4 = (bf16[2,2,16,128]{3,2,0,1:T(8,128)(2,1)S(1)}, bf16[2,2,16,128]{3,2,0,1:T(8,128)(2,1)S(1)}, u32[]{:S(2)}, u32[]{:S(2)}) collective-permute-start(bf16[2,2,16,128]{3,2,0,1:T(8,128)(2,1)S(1)} %get-tuple-element.19), channel_id=1, source_target_pairs={{0,17},{1,16},{2,19},{3,18},{4,21},{5,20},{6,23},{7,22},{8,25},{9,... | collective-permute-start | bytes 49160 | tf_op jit(solution)/shard_map/ppermute | solution.py:271
  15.7 1.4 %collective-permute-done.4 = bf16[2,2,16,128]{3,2,0,1:T(8,128)(2,1)S(1)} collective-permute-done((bf16[2,2,16,128]{3,2,0,1:T(8,128)(2,1)S(1)}, bf16[2,2,16,128]{3,2,0,1:T(8,128)(2,1)S(1)}, u32[]{:S(2)}, u32[]{:S(2)}) %collective-permute-start.4) | collective-permute-done | bytes 16416 | tf_op jit(solution)/shard_map/ppermute | solution.py:271
  17.2 1.6 %collective-permute-start.5 = (bf16[4,16,128]{2,1,0:T(8,128)(2,1)S(1)}, bf16[4,16,128]{2,1,0:T(8,128)(2,1)S(1)}, u32[]{:S(2)}, u32[]{:S(2)}) collective-permute-start(bf16[4,16,128]{2,1,0:T(8,128)(2,1)S(1)} %get-tuple-element.17), channel_id=1, source_target_pairs={{0,5},{1,4},{2,7},{3,6},{4,1},{5,0},{6,3},{7,2},{8,13},{9,12},{10,... | collective-permute-start | bytes 49160 | tf_op jit(solution)/shard_map/ppermute | solution.py:271
  18.8 0.7 %spread.2.refs_1_ = bf16[64,16,128]{2,1,0:T(8,128)(2,1)} custom-call(f32[16,128]{1,0:T(8,128)S(1)} %get-tuple-element.8.j_in, f32[64,128]{1,0:T(8,128)S(1)} %get-tuple-element.9.i_in, bf16[4,16,128]{2,1,0:T(8,128)(2,1)S(1)} %get-tuple-element.16.refs_0_), custom_call_target="tpu_custom_call" | custom-call | flops 1000000 | bytes 131072 | tf_op jit(solution)/shard_map/spread/pallas_call | solution.py:218
  19.6 0.9 %collective-permute-done.5.refs_0_ = bf16[4,16,128]{2,1,0:T(8,128)(2,1)S(1)} collective-permute-done((bf16[4,16,128]{2,1,0:T(8,128)(2,1)S(1)}, bf16[4,16,128]{2,1,0:T(8,128)(2,1)S(1)}, u32[]{:S(2)}, u32[]{:S(2)}) %collective-permute-start.5) | collective-permute-done | bytes 16416 | tf_op jit(solution)/shard_map/ppermute | solution.py:271
  20.4 0.7 %spread.3 = bf16[64,16,128]{2,1,0:T(8,128)(2,1)} custom-call(f32[16,128]{1,0:T(8,128)S(1)} %get-tuple-element.8.j_in, f32[64,128]{1,0:T(8,128)S(1)} %get-tuple-element.9.i_in, bf16[4,16,128]{2,1,0:T(8,128)(2,1)S(1)} %collective-permute-done.5.refs_0_, bf16[64,16,128]{2,1,0:T(8,128)(2,1)} %spread.2.refs_1_), custom_call_target="tpu_custom_call", output_to_operand_aliasing={{}: (3, {})} | custom-call | flops 1000000 | bytes 131072 | tf_op jit(solution)/shard_map/spread/pallas_call | solution.py:218
  (9 shorter events, 0.1 us)
Async XLA Ops:
  4.0 1.5 %collective-permute-start = (f32[2,2,2,2,16,128]{5,4,2,3,1,0:T(8,128)S(1)}, f32[2,2,2,2,16,128]{5,4,2,3,1,0:T(8,128)S(1)}, u32[]{:S(2)}, u32[]{:S(2)}) collective-permute-start(f32[2,2,2,2,16,128]{5,4,2,3,1,0:T(8,128)S(1)} %copy.7), channel_id=1, source_target_pairs={{0,1},{1,0},{2,3},{3,2},{4,5},{5,4},{6,7},{7,6},{8,9},{9,8},{10,11... | collective-permute-start | bytes 393224 | tf_op jit(solution)/shard_map/ppermute | solution.py:271
  5.5 4.8 %collective-permute-start.1 = (f32[2,2,16,128]{3,2,0,1:T(8,128)S(1)}, f32[2,2,16,128]{3,2,0,1:T(8,128)S(1)}, u32[]{:S(2)}, u32[]{:S(2)}) collective-permute-start(f32[2,2,16,128]{3,2,0,1:T(8,128)S(1)} %get-tuple-element.13), channel_id=1, source_target_pairs={{0,2},{1,3},{2,0},{3,1},{4,6},{5,7},{6,4},{7,5},{8,10},{9,11},{10,... | collective-permute-start | bytes 98312 | tf_op jit(solution)/shard_map/ppermute | solution.py:271
  8.5 4.5 %collective-permute-start.3 = (f32[2,2,16,128]{3,2,0,1:T(8,128)S(1)}, f32[2,2,16,128]{3,2,0,1:T(8,128)S(1)}, u32[]{:S(2)}, u32[]{:S(2)}) collective-permute-start(f32[2,2,16,128]{3,2,0,1:T(8,128)S(1)} %get-tuple-element.14), channel_id=1, source_target_pairs={{0,11},{1,10},{2,9},{3,8},{4,15},{5,14},{6,13},{7,12},{8,3},{9,2},... | collective-permute-start | bytes 98312 | tf_op jit(solution)/shard_map/ppermute | solution.py:271
  9.5 3.5 %collective-permute-start.2 = (f32[2,2,16,128]{3,2,0,1:T(8,128)S(1)}, f32[2,2,16,128]{3,2,0,1:T(8,128)S(1)}, u32[]{:S(2)}, u32[]{:S(2)}) collective-permute-start(f32[2,2,16,128]{3,2,0,1:T(8,128)S(1)} %get-tuple-element.15), channel_id=1, source_target_pairs={{0,9},{1,8},{2,11},{3,10},{4,13},{5,12},{6,15},{7,14},{8,1},{9,0},... | collective-permute-start | bytes 98312 | tf_op jit(solution)/shard_map/ppermute | solution.py:271
  13.0 4.2 %collective-permute-start.4 = (bf16[2,2,16,128]{3,2,0,1:T(8,128)(2,1)S(1)}, bf16[2,2,16,128]{3,2,0,1:T(8,128)(2,1)S(1)}, u32[]{:S(2)}, u32[]{:S(2)}) collective-permute-start(bf16[2,2,16,128]{3,2,0,1:T(8,128)(2,1)S(1)} %get-tuple-element.19), channel_id=1, source_target_pairs={{0,17},{1,16},{2,19},{3,18},{4,21},{5,20},{6,23},{7,22},{8,25},{9,... | collective-permute-start | bytes 49160 | tf_op jit(solution)/shard_map/ppermute | solution.py:271
  17.2 3.2 %collective-permute-start.5 = (bf16[4,16,128]{2,1,0:T(8,128)(2,1)S(1)}, bf16[4,16,128]{2,1,0:T(8,128)(2,1)S(1)}, u32[]{:S(2)}, u32[]{:S(2)}) collective-permute-start(bf16[4,16,128]{2,1,0:T(8,128)(2,1)S(1)} %get-tuple-element.17), channel_id=1, source_target_pairs={{0,5},{1,4},{2,7},{3,6},{4,1},{5,0},{6,3},{7,2},{8,13},{9,12},{10,... | collective-permute-start | bytes 49160 | tf_op jit(solution)/shard_map/ppermute | solution.py:271
